TPU v7x, 256 devices: a whole 4x4x8 slice. The times are simulated.
256 devices in a mesh: rows: 256 (over x, z, y, core).
Axes of the slice: x: 4, y: 4, z: 8, core: 2. Of those that a mesh axis runs over, the one named last changes fastest.
Arguments:
- vectors: bfloat16 [8, 2097152], P(None, 'rows'), may hold values from -6 to 6
- basis_leaf: bfloat16 [32, 2097152], P(None, 'rows'), may hold values from -0.75 to 0.75
- near_block: bfloat16 [6, 64, 2097152], P(None, None, 'rows'), may hold values from -0.3125 to 0.3125
- near_index: int32 [6, 32768], P(None, 'rows'), may hold values from 0 to 32767, as said below
- near_count: int32 [32768], P('rows'), may hold values from 1 to 6
- leaf_trans: bfloat16 [32, 32, 32768], P(None, None, 'rows'), may hold values from -0.5 to 0.5
- leaf_coupling: bfloat16 [8, 32, 32, 32768], P(None, None, None, 'rows'), may hold values from -0.375 to 0.375
- leaf_index: int32 [8, 32768], P(None, 'rows'), may hold values from 0 to 32767, as said below
- cluster_trans: bfloat16 [32, 32, 4096], P(None, None, 'rows'), may hold values from -0.5 to 0.5
- cluster_coupling: bfloat16 [3, 32, 32, 4096], P(None, None, None, 'rows'), may hold values from -0.625 to 0.625
- cluster_index: int32 [3, 4096], P(None, 'rows'), may hold values from 0 to 4095, as said below
- cluster_count: int32 [4096], P('rows'), may hold values from 1 to 3, as said below
- middle_trans: bfloat16 [32, 32, 512], P(None, None, 'rows'), may hold values from -0.5 to 0.5
- middle_coupling: bfloat16 [8, 32, 32, 512], P(None, None, None, 'rows'), may hold values from -0.375 to 0.375
- middle_index: int32 [8, 512], P(None, 'rows'), may hold values from 0 to 511, as said below
- middle_count: int32 [512], P('rows'), may hold values from 1 to 8
- top_coupling: bfloat16 [8, 32, 32, 64], replicated, may hold values from -0.375 to 0.375
- top_index: int32 [8, 64], replicated, may hold values from 0 to 63, as said below
Outputs:
- product: bfloat16 [8, 2097152], P(None, 'rows')
Inputs may be any that keep to these rules, and one draw needn't show every extreme that they name: near_index[s, i] is a leaf within 4 leaves of leaf i; slot 0 is i itself; the first near_count[i] slots are distinct. leaf_index[s, i] lies in the second-level clusters k - 2 to k + 2, k the cluster of leaf i, and more than 4 leaves from i; distinct over s. cluster_index[s, k] is a cluster within 2 clusters of k, not k; the first slots hold k + 1 and then k - 1, those of them that exist; the first cluster_count[k] slots are distinct. cluster_count[k] is 2 or more wherever k has two or more partners within reach, except for cluster 0. middle_index[s, j] is any cluster of that level but j; the first middle_count[j] slots are distinct. top_index[s, g] are distinct top clusters other than g.
All inputs are finite; a program needn't handle non-finite values.
Results may differ from a plain program's by a relative error of at most 0.01.
Values may be sent and summed in bfloat16 or wider, within the bound.
No kernel may reach another device: no remote copies, remote signals or barrier semaphores. Data moves between devices by JAX's collectives and lax.ppermute only.
A program may use at most 128 MiB of HBM per device.

v0:
```python
import jax
import jax.numpy as jnp
from jax import lax
from jax.sharding import PartitionSpec as P

LEAF = 64
BRANCH = 8
NEARW = 4
FARW = 2


def extended(cells, sides, width):
    for axis, dim in sides:
        count = lax.axis_size(axis)
        ends = count - 1
        head = lax.slice_in_dim(cells, 0, width, axis=dim)
        tail = lax.slice_in_dim(cells, cells.shape[dim] - width, cells.shape[dim], axis=dim)
        cells = jnp.concatenate(
            [
                lax.ppermute(tail, axis, [(i, (i + 1) % count) for i in range(ends)]),
                cells,
                lax.ppermute(head, axis, [((i + 1) % count, i) for i in range(ends)]),
            ],
            axis=dim,
        )
    return cells


def upward(children, transfer):
    products = jnp.einsum("vrn,rqn->vqn", children, transfer, preferred_element_type=jnp.float32)
    return products.reshape(products.shape[0], products.shape[1], -1, BRANCH).sum(axis=3)


def select(positions, usable, span_size):
    onehot = (positions[..., None] == jnp.arange(span_size, dtype=jnp.int32)) & usable[..., None]
    return onehot.astype(jnp.bfloat16)


def body(
    vectors,
    basis_leaf,
    near_block,
    near_index,
    near_count,
    leaf_trans,
    leaf_coupling,
    leaf_index,
    cluster_trans,
    cluster_coupling,
    cluster_index,
    cluster_count,
    middle_trans,
    middle_coupling,
    middle_index,
    middle_count,
    top_coupling,
    top_index,
):
    columns = vectors.shape[0]
    leaves = vectors.shape[1] // LEAF
    basis_rank = basis_leaf.shape[0]
    clusters = leaves // BRANCH
    device = lax.axis_index("rows")
    devices = lax.axis_size("rows")
    group_size = BRANCH**3 // leaves
    top_count = devices // group_size
    owner_group = device // group_size
    leaf_first = device * leaves
    local_leaves = vectors.reshape(columns, leaves, LEAF)
    local_basis = basis_leaf.reshape(basis_rank, leaves, LEAF)
    coef_leaf = jnp.einsum(
        "via,ria->vri", local_leaves, local_basis, preferred_element_type=jnp.float32
    ).astype(jnp.bfloat16)
    coef_cluster = upward(coef_leaf, leaf_trans).astype(jnp.bfloat16)
    coef_middle = upward(coef_cluster, cluster_trans).astype(jnp.bfloat16)
    middle_slots = middle_index.shape[0]
    middle_usable = jnp.arange(middle_slots, dtype=jnp.int32)[:, None] < middle_count[None, :]
    shard_coef = lax.all_gather(coef_middle, "rows", axis=2, tiled=True)
    width_here = shard_coef.shape[2]
    onehot = select(middle_index, middle_usable, width_here)
    picked_middle = jnp.einsum(
        "vrc,sjc->svrj", shard_coef, onehot, preferred_element_type=jnp.float32
    )
    partial_top = jnp.einsum(
        "vrj,rqj->vq", coef_middle, middle_trans, preferred_element_type=jnp.float32
    )
    slot_hit = (jnp.arange(top_count, dtype=jnp.int32) == owner_group).astype(jnp.float32)
    slot_table = partial_top[:, None, :] * slot_hit[None, :, None]
    coef_top = lax.psum(slot_table, "rows").astype(jnp.bfloat16)
    halo_leaf = extended(coef_leaf, (("rows", 2),), BRANCH * FARW)
    halo_cluster = extended(coef_cluster, (("rows", 2),), FARW)
    halo_points = extended(vectors, (("rows", 1),), NEARW * LEAF)
    top_column = lax.dynamic_index_in_dim(top_index, owner_group, 1, keepdims=False)
    top_onehot = (top_column[:, None] == jnp.arange(top_count, dtype=jnp.int32)[None, :]).astype(
        jnp.bfloat16
    )
    picked_top = jnp.einsum(
        "vgr,sg->svr", coef_top, top_onehot, preferred_element_type=jnp.float32
    ).astype(jnp.bfloat16)
    couplings_top = lax.dynamic_index_in_dim(top_coupling, owner_group, 3, keepdims=False)
    field_top = jnp.einsum(
        "svr,srq->vq", picked_top, couplings_top, preferred_element_type=jnp.float32
    ).astype(jnp.bfloat16)
    middle_near = jnp.einsum(
        "svrj,srqj->vqj",
        picked_middle.astype(jnp.bfloat16),
        middle_coupling,
        preferred_element_type=jnp.float32,
    )
    middle_down = jnp.einsum(
        "vq,rqj->vrj", field_top, middle_trans, preferred_element_type=jnp.float32
    )
    field_middle = (middle_near + middle_down).astype(jnp.bfloat16)
    cluster_slots = cluster_index.shape[0]
    cluster_usable = jnp.arange(cluster_slots, dtype=jnp.int32)[:, None] < cluster_count[None, :]
    cluster_onehot = select(
        cluster_index - device * clusters + FARW, cluster_usable, halo_cluster.shape[2]
    )
    picked_cluster = jnp.einsum(
        "vrh,skh->svrk", halo_cluster, cluster_onehot, preferred_element_type=jnp.float32
    ).astype(jnp.bfloat16)
    cluster_near = jnp.einsum(
        "svrk,srqk->vqk", picked_cluster, cluster_coupling, preferred_element_type=jnp.float32
    )
    cluster_down = jnp.einsum(
        "vqk,rqk->vrk",
        jnp.repeat(field_middle, BRANCH, axis=2),
        cluster_trans,
        preferred_element_type=jnp.float32,
    )
    field_cluster = (cluster_near + cluster_down).astype(jnp.bfloat16)
    leaf_slots = leaf_index.shape[0]
    span_clusters = 2 * FARW + 1
    halo_grouped = halo_leaf.reshape(columns, basis_rank, clusters + 2 * FARW, BRANCH)
    leaf_window = jnp.concatenate(
        [halo_grouped[:, :, offset : offset + clusters, :] for offset in range(span_clusters)],
        axis=3,
    )
    leaf_ids = jnp.arange(leaves, dtype=jnp.int32)
    window_start = leaf_first + (leaf_ids // BRANCH - FARW) * BRANCH
    leaf_usable = jnp.ones(leaf_index.shape, jnp.bool_)
    leaf_onehot = select(leaf_index - window_start[None, :], leaf_usable, span_clusters * BRANCH)
    leaf_onehot = leaf_onehot.reshape(leaf_slots, clusters, BRANCH, span_clusters * BRANCH)
    picked_leaf = jnp.einsum(
        "vrcw,scmw->svrcm", leaf_window, leaf_onehot, preferred_element_type=jnp.float32
    ).astype(jnp.bfloat16)
    picked_leaf = picked_leaf.reshape(leaf_slots, columns, basis_rank, leaves)
    leaf_near = jnp.einsum(
        "svri,srqi->vqi", picked_leaf, leaf_coupling, preferred_element_type=jnp.float32
    )
    leaf_down = jnp.einsum(
        "vqi,rqi->vri",
        jnp.repeat(field_cluster, BRANCH, axis=2),
        leaf_trans,
        preferred_element_type=jnp.float32,
    )
    field_leaf = (leaf_near + leaf_down).astype(jnp.bfloat16)
    near_slots = near_index.shape[0]
    near_span = 2 * NEARW + 1
    halo_leaves = halo_points.reshape(columns, leaves + 2 * NEARW, LEAF)
    near_window = jnp.stack(
        [halo_leaves[:, offset : offset + leaves, :] for offset in range(near_span)], axis=0
    )
    near_usable = jnp.arange(near_slots, dtype=jnp.int32)[:, None] < near_count[None, :]
    near_offset = near_index - leaf_first - leaf_ids[None, :] + NEARW
    near_weight = (
        near_offset[:, None, :] == jnp.arange(near_span, dtype=jnp.int32)[None, :, None]
    ) & near_usable[:, None, :]
    near_weight = near_weight.astype(jnp.bfloat16)
    picked_near = jnp.einsum(
        "dvib,sdi->svib", near_window, near_weight, preferred_element_type=jnp.float32
    ).astype(jnp.bfloat16)
    blocks = near_block.reshape(near_slots, LEAF, leaves, LEAF)
    near_part = jnp.einsum(
        "svib,sbia->via", picked_near, blocks, preferred_element_type=jnp.float32
    )
    far_part = jnp.einsum(
        "vri,ria->via", field_leaf, local_basis, preferred_element_type=jnp.float32
    )
    return (near_part + far_part).reshape(columns, -1).astype(jnp.bfloat16)


def solution(mesh):
    in_specs = (
        P(None, "rows"),
        P(None, "rows"),
        P(None, None, "rows"),
        P(None, "rows"),
        P("rows"),
        P(None, None, "rows"),
        P(None, None, None, "rows"),
        P(None, "rows"),
        P(None, None, "rows"),
        P(None, None, None, "rows"),
        P(None, "rows"),
        P("rows"),
        P(None, None, "rows"),
        P(None, None, None, "rows"),
        P(None, "rows"),
        P("rows"),
        P(),
        P(),
    )
    out_specs = P(None, "rows")
    return jax.shard_map(body, mesh=mesh, in_specs=in_specs, out_specs=out_specs, check_vma=False)
```

profile of v0, /device:TPU:1, one launch (start us, length us, event | category | flops | bytes accessed | tf_op | source)
XLA Modules:
  0.0 349.0 jit_solution(6162285271056953822)
XLA Ops:
  0.0 2.9 reshape.116
  2.9 1.9 reshape.117
  6.3 2.2 fusion.15
  9.5 4.6 %collective-permute-start.4 = (bf16[8,32,2]{1,2,0:T(2,128)(2,1)}, bf16[8,32,2]{1,2,0:T(2,128)(2,1)}, u32[]{:S(2)}, u32[]{:S(2)}) collective-permute-start(bf16[8,32,2]{1,2,0:T(2,128)(2,1)} %get-tuple-element.23), channel_id=1, source_target_pairs={{0,1},{1,2},{2,3},{3,4},{4,5},{5,6},{6,7},{7,8},{8,9},{9,10},{10,1... | collective-permute-start | bytes 3080 | tf_op jit(solution)/shard_map/ppermute | solution.py:20
  14.1 2.4 collective-permute-start.5
  17.2 3.1 collective-permute-start
  20.3 1.9 collective-permute-start.1
  22.9 3.6 %collective-permute-start.2 = (bf16[8,32,16]{1,0,2:T(8,128)(2,1)}, bf16[8,32,16]{1,0,2:T(8,128)(2,1)}, u32[]{:S(2)}, u32[]{:S(2)}) collective-permute-start(bf16[8,32,16]{1,0,2:T(8,128)(2,1)} %get-tuple-element.19), channel_id=1, source_target_pairs={{0,1},{1,2},{2,3},{3,4},{4,5},{5,6},{6,7},{7,8},{8,9},{9,10},{10,1... | collective-permute-start | bytes 24584 | tf_op jit(solution)/shard_map/ppermute | solution.py:20
  26.7 75.3 %all_gather.3 = bf16[8,32,512]{1,0,2:T(8,128)(2,1)} all-gather(bf16[8,32,2]{1,0,2:T(8,128)(2,1)S(1)} %bitcast_reduce_fusion.1), channel_id=1, replica_groups=mesh['rows'=256] {'rows'}, dimensions={2}, use_global_device_ids=true | all-gather | bytes 263168 | tf_op jit(solution)/shard_map/all_gather | solution.py:78
  102.3 74.2 %psum.7 = bf16[8,64,32]{1,2,0:T(8,128)(2,1)} all-reduce(f32[8,64,32]{1,2,0:T(8,128)S(1)} %broadcast_multiply_fusion), channel_id=1, replica_groups=mesh['rows'=256] {'rows'}, use_global_device_ids=true, to_apply=%region_2.3 | all-reduce | flops 16384 | bytes 98304 | tf_op jit(solution)/shard_map/psum | solution.py:89
  177.2 2.0 constant_dynamic-slice_fusion
  179.2 2.9 copy.261
  194.3 17.9 %reshape.115 = bf16[6,64,128,64]{3,2,1,0:T(8,128)(2,1)} reshape(bf16[6,64,8192]{2,1,0:T(8,128)(2,1)} %param.20) | data formatting | bytes 12582912 | tf_op jit(solution)/shard_map/reshape | solution.py:173
  213.0 12.6 %copy.222 = bf16[8,32,32,128]{2,1,0,3:T(8,128)(2,1)} copy(bf16[8,32,32,128]{3,2,1,0:T(8,128)(2,1)} %param.24) | data formatting | bytes 4194304 | tf_op args[6]
  225.5 13.5 %collective-permute-start.3 = (bf16[8,32,16]{1,0,2:T(8,128)(2,1)}, bf16[8,32,16]{1,0,2:T(8,128)(2,1)}, u32[]{:S(2)}, u32[]{:S(2)}) collective-permute-start(bf16[8,32,16]{1,0,2:T(8,128)(2,1)} %get-tuple-element.20), channel_id=1, source_target_pairs={{1,0},{2,1},{3,2},{4,3},{5,4},{6,5},{7,6},{8,7},{9,8},{10,9},{11,1... | collective-permute-start | bytes 24584 | tf_op jit(solution)/shard_map/ppermute | solution.py:22
  248.8 1.7 copy.200
  250.5 1.7 copy.201
  252.3 1.7 copy.202
  254.0 1.7 copy.203
  255.7 1.7 copy.204
  257.4 1.7 copy.205
  272.7 7.5 %copy.208 = bf16[9,8,128,64]{3,0,1,2:T(8,128)(2,1)} copy(bf16[9,8,128,64]{2,3,1,0:T(8,128)(2,1)} %bitcast_dynamic-update-slice_fusion) | data formatting | bytes 2359296 | tf_op jit(solution)/shard_map/stack | solution.py:161
  280.2 3.0 convert_bitcast_fusion.1
  283.2 30.1 %fusion.5 = f32[128,8,64]{2,1,0:T(8,128)} fusion(bf16[6,64,128,64]{3,2,1,0:T(8,128)(2,1)} %reshape.115, bf16[6,8,128,64]{3,0,1,2:T(8,128)(2,1)S(1)} %convert_bitcast_fusion.1), kind=kOutput, calls=%fused_computation.8 | convolution fusion | flops 50331648 | bytes 7340032 | tf_op jit(solution)/shard_map/svib,sbia->via/dot_general | solution.py:174
  315.4 2.3 copy.256
  317.6 2.3 copy.257
  319.9 2.4 copy.258
  322.3 2.3 copy.259
  326.0 6.7 %concatenate.14 = bf16[8,32,16,40]{3,1,0,2:T(8,128)(2,1)} concatenate(bf16[8,32,16,8]{3,1,0,2:T(8,128)(2,1)} %copy.256, bf16[8,32,16,8]{3,1,0,2:T(8,128)(2,1)} %copy.257, bf16[8,32,16,8]{3,1,0,2:T(8,128)(2,1)} %copy.258, bf16[8,32,16,8]{3,1,0,2:T(8,128)(2,1)} %copy.259, bf16[8,32,16,8]{3,1,0,2:T(8,128)(2,1)} %copy.260), dimensions={3} | concatenate | bytes 655360 | tf_op jit(solution)/shard_map/concatenate | solution.py:135
  332.7 3.0 convert_bitcast_fusion
  336.3 7.0 %fusion.10 = f32[128,8,32]{2,1,0:T(8,128)} fusion(bf16[8,32,32,128]{2,1,0,3:T(8,128)(2,1)} %copy.222, bf16[8,8,32,128]{2,3,1,0:T(8,128)(2,1)S(1)} %bitcast.130), kind=kOutput, calls=%fused_computation.11 | convolution fusion | flops 16777216 | bytes 2752512 | tf_op jit(solution)/shard_map/svri,srqi->vqi/dot_general | solution.py:148
  343.4 3.5 %fusion.16 = bf16[8,128,64]{2,0,1:T(8,128)(2,1)} fusion(f32[128,8,64]{2,1,0:T(8,128)} %fusion.5, f32[128,8,32]{2,1,0:T(8,128)} %fusion.10, bf16[32,32,128]{1,0,2:T(8,128)(2,1)S(1)} %copy.223, bf16[32,128,64]{2,1,0:T(8,128)(2,1)} %reshape.116, bf16[8,32,128]{1,2,0:T(8,128)(2,1)S(1)} %copy-done.3), kind=kOutput, calls=%fused_computation.16 | convolution fusion | flops 6488064 | bytes 1376256 | tf_op jit(solution)/shard_map/vri,ria->via/dot_general | solution.py:177
  (92 shorter events, 47.0 us)
Async XLA Ops:
  0.0 177.2 %copy-start = (bf16[8,32,32,64]{3,2,1,0:T(8,128)(2,1)S(1)}, bf16[8,32,32,64]{3,2,1,0:T(8,128)(2,1)}, u32[]{:S(2)}) copy-start(bf16[8,32,32,64]{3,2,1,0:T(8,128)(2,1)} %param.34) | copy-start | bytes 3145732
  0.0 4.8 %copy-start.7 = (bf16[32,32,128]{2,1,0:T(8,128)(2,1)S(1)}, bf16[32,32,128]{2,1,0:T(8,128)(2,1)}, u32[]{:S(2)}) copy-start(bf16[32,32,128]{2,1,0:T(8,128)(2,1)} %param.23) | copy-start | bytes 786436
  4.8 11.7 %copy-start.5 = (bf16[8,8192]{1,0:T(8,128)(2,1)S(1)}, bf16[8,8192]{1,0:T(8,128)(2,1)}, u32[]{:S(2)}) copy-start(bf16[8,8192]{1,0:T(8,128)(2,1)} %param.18) | copy-start | bytes 393220
  6.3 20.3 %copy-start.9 = (bf16[32,32,16]{1,2,0:T(8,128)(2,1)S(1)}, bf16[32,32,16]{1,2,0:T(8,128)(2,1)}, u32[]{:S(2)}) copy-start(bf16[32,32,16]{1,2,0:T(8,128)(2,1)} %param.26) | copy-start | bytes 98308
  6.3 95.7 %copy-start.11 = (bf16[32,32,2]{1,2,0:T(2,128)(2,1)S(1)}, bf16[32,32,2]{1,2,0:T(2,128)(2,1)}, u32[]{:S(2)}) copy-start(bf16[32,32,2]{1,2,0:T(2,128)(2,1)} %param.30) | copy-start | bytes 12292
  6.3 170.2 %copy-start.14 = (s32[8,64]{1,0:T(8,128)S(1)}, s32[8,64]{1,0:T(8,128)}, u32[]{:S(2)}) copy-start(s32[8,64]{1,0:T(8,128)} %param.35) | copy-start | bytes 6148
  8.5 13.7 %copy-start.1 = (bf16[8,32,128]{1,0,2:T(8,128)(2,1)}, bf16[8,32,128]{1,0,2:T(8,128)(2,1)S(1)}, u32[]{:S(2)}) copy-start(bf16[8,32,128]{1,0,2:T(8,128)(2,1)S(1)} %fusion.15) | copy-start | bytes 196612
  8.9 93.1 %copy-start.12 = (bf16[8,32,16]{1,2,0:T(8,128)(2,1)}, bf16[8,32,16]{1,2,0:T(8,128)(2,1)S(1)}, u32[]{:S(2)}) copy-start(bf16[8,32,16]{1,2,0:T(8,128)(2,1)S(1)} %copy.314) | copy-start | bytes 24580
  9.5 216.0 %collective-permute-start.4 = (bf16[8,32,2]{1,2,0:T(2,128)(2,1)}, bf16[8,32,2]{1,2,0:T(2,128)(2,1)}, u32[]{:S(2)}, u32[]{:S(2)}) collective-permute-start(bf16[8,32,2]{1,2,0:T(2,128)(2,1)} %get-tuple-element.23), channel_id=1, source_target_pairs={{0,1},{1,2},{2,3},{3,4},{4,5},{5,6},{6,7},{7,8},{8,9},{9,10},{10,1... | collective-permute-start | bytes 3080 | tf_op jit(solution)/shard_map/ppermute | solution.py:20
  14.1 224.9 %collective-permute-start.5 = (bf16[8,32,2]{1,2,0:T(2,128)(2,1)}, bf16[8,32,2]{1,2,0:T(2,128)(2,1)}, u32[]{:S(2)}, u32[]{:S(2)}) collective-permute-start(bf16[8,32,2]{1,2,0:T(2,128)(2,1)} %get-tuple-element.24), channel_id=1, source_target_pairs={{1,0},{2,1},{3,2},{4,3},{5,4},{6,5},{7,6},{8,7},{9,8},{10,9},{11,1... | collective-permute-start | bytes 3080 | tf_op jit(solution)/shard_map/ppermute | solution.py:22
  17.2 225.7 %collective-permute-start = (bf16[8,256]{1,0:T(8,128)(2,1)}, bf16[8,256]{1,0:T(8,128)(2,1)}, u32[]{:S(2)}, u32[]{:S(2)}) collective-permute-start(bf16[8,256]{1,0:T(8,128)(2,1)} %get-tuple-element.21), channel_id=1, source_target_pairs={{0,1},{1,2},{2,3},{3,4},{4,5},{5,6},{6,7},{7,8},{8,9},{9,10},{10,1... | collective-permute-start | bytes 12296 | tf_op jit(solution)/shard_map/ppermute | solution.py:20
  20.3 222.6 %collective-permute-start.1 = (bf16[8,256]{1,0:T(8,128)(2,1)}, bf16[8,256]{1,0:T(8,128)(2,1)}, u32[]{:S(2)}, u32[]{:S(2)}) collective-permute-start(bf16[8,256]{1,0:T(8,128)(2,1)} %get-tuple-element.22), channel_id=1, source_target_pairs={{1,0},{2,1},{3,2},{4,3},{5,4},{6,5},{7,6},{8,7},{9,8},{10,9},{11,1... | collective-permute-start | bytes 12296 | tf_op jit(solution)/shard_map/ppermute | solution.py:22
  22.9 290.4 %collective-permute-start.2 = (bf16[8,32,16]{1,0,2:T(8,128)(2,1)}, bf16[8,32,16]{1,0,2:T(8,128)(2,1)}, u32[]{:S(2)}, u32[]{:S(2)}) collective-permute-start(bf16[8,32,16]{1,0,2:T(8,128)(2,1)} %get-tuple-element.19), channel_id=1, source_target_pairs={{0,1},{1,2},{2,3},{3,4},{4,5},{5,6},{6,7},{7,8},{8,9},{9,10},{10,1... | collective-permute-start | bytes 24584 | tf_op jit(solution)/shard_map/ppermute | solution.py:20
  179.2 2.9 copy-start.16
  179.2 3.5 %copy-start.15 = (s32[6,128]{1,0:T(8,128)S(1)}, s32[6,128]{1,0:T(8,128)}, u32[]{:S(2)}) copy-start(s32[6,128]{1,0:T(8,128)} %param.21) | copy-start | bytes 9220
  179.2 4.9 %copy-start.10 = (bf16[8,64,32]{1,2,0:T(8,128)(2,1)S(1)}, bf16[8,64,32]{1,2,0:T(8,128)(2,1)}, u32[]{:S(2)}) copy-start(bf16[8,64,32]{1,2,0:T(8,128)(2,1)} %psum.7) | copy-start | bytes 98308
  213.0 26.1 %copy-start.13 = (bf16[8,32,16]{1,2,0:T(8,128)(2,1)S(1)}, bf16[8,32,16]{1,2,0:T(8,128)(2,1)}, u32[]{:S(2)}) copy-start(bf16[8,32,16]{1,2,0:T(8,128)(2,1)} %copy-done.12) | copy-start | bytes 24580
  225.5 87.8 %collective-permute-start.3 = (bf16[8,32,16]{1,0,2:T(8,128)(2,1)}, bf16[8,32,16]{1,0,2:T(8,128)(2,1)}, u32[]{:S(2)}, u32[]{:S(2)}) collective-permute-start(bf16[8,32,16]{1,0,2:T(8,128)(2,1)} %get-tuple-element.20), channel_id=1, source_target_pairs={{1,0},{2,1},{3,2},{4,3},{5,4},{6,5},{7,6},{8,7},{9,8},{10,9},{11,1... | collective-permute-start | bytes 24584 | tf_op jit(solution)/shard_map/ppermute | solution.py:22
  247.0 13.2 %copy-start.4 = (bf16[8,128,64]{2,1,0:T(8,128)(2,1)S(1)}, bf16[8,128,64]{2,1,0:T(8,128)(2,1)}, u32[]{:S(2)}) copy-start(bf16[8,128,64]{2,1,0:T(8,128)(2,1)} %get-tuple-element.10) | copy-start | bytes 393220
  272.7 7.5 %copy-start.6 = (s32[6,128]{0,1:T(8,128)S(1)}, s32[6,128]{0,1:T(8,128)}, u32[]{:S(2)}) copy-start(s32[6,128]{0,1:T(8,128)} %copy.198) | copy-start | bytes 9220
  283.2 30.1 %copy-start.2 = (bf16[8,32,128]{1,0,2:T(8,128)(2,1)S(1)}, bf16[8,32,128]{1,0,2:T(8,128)(2,1)}, u32[]{:S(2)}) copy-start(bf16[8,32,128]{1,0,2:T(8,128)(2,1)} %copy-done.1) | copy-start | bytes 196612
  326.0 6.7 %copy-start.8 = (s32[8,16,8]{2,0,1:T(8,128)S(1)}, s32[8,16,8]{2,0,1:T(8,128)}, u32[]{:S(2)}) copy-start(s32[8,16,8]{2,0,1:T(8,128)} %copy.211) | copy-start | bytes 12292
  336.3 7.1 %copy-start.3 = (bf16[8,32,128]{1,2,0:T(8,128)(2,1)S(1)}, bf16[8,32,128]{1,2,0:T(8,128)(2,1)}, u32[]{:S(2)}) copy-start(bf16[8,32,128]{1,2,0:T(8,128)(2,1)} %broadcast_bitcast_fusion) | copy-start | bytes 196612
where the time goes:
time: 355 us; the launch traced here: 349 us
  blocking collectives  149 us (42%)
  local copies, waits for them, and re-layouts  105 us (30%)
  matrix products  57.7 us (16%)
  starting transfers between devices  29.2 us (8%)
  other arithmetic  7.36 us (2%)
    all_gather x1, blocking collectives, body(): shard_coef = lax.all_gather(coef_middle, 'rows', axis=2, tiled=True)  75.3 us
    psum x1, blocking collectives, body(): coef_top = lax.psum(slot_table, 'rows').astype(jnp.bfloat16)  74.2 us
    unnamed x50, local copies, waits for them, and re-layouts  38.4 us
    dot_general x1, matrix products, body(): jnp.einsum('svib,sbia->via', picked_near, blocks, preferred_element_type=...  30.1 us
    reshape x1, local copies, waits for them, and re-layouts, body(): blocks = near_block.reshape(near_slots, LEAF, leaves, LEAF)  17.9 us
    ppermute x3, starting transfers between devices, extended(): lax.ppermute(head, axis, [((i + 1) % count, i) for i in range(ends)])  17.8 us
    slice x10, local copies, waits for them, and re-layouts, body(): halo_leaves[:, offset:offset + leaves, :]  15 us
    ppermute x3, starting transfers between devices, extended(): lax.ppermute(tail, axis, [(i, (i + 1) % count) for i in range(ends)])  11.4 us
  transfers between devices with their start and end apart: 6, of which 0 were waited for; matrix products, arithmetic and copies ran while one was open for 36% of the time, Pallas kernels for 0%

commit v1 on v0

v1 whole, which is shorter than its diff:
```python
import jax
import jax.numpy as jnp
from jax import lax
from jax.experimental import pallas as pl
from jax.experimental.pallas import tpu as pltpu
from jax.sharding import PartitionSpec as P

F32 = jnp.float32
BF = jnp.bfloat16
I32 = jnp.int32
NT = (((1,), (1,)), ((), ()))
MIB = 1 << 20


def iota(shape, dim):
    return lax.broadcasted_iota(I32, shape, dim)


def mm(a, b):
    return jnp.dot(a, b, preferred_element_type=F32)


def mm_nt(a, b):
    return lax.dot_general(a, b, NT, preferred_element_type=F32)


def halves(x):
    hi = x.astype(BF)
    return hi, (x - hi.astype(F32)).astype(BF)


def fetch(sems, *pairs):
    copies = [pltpu.make_async_copy(a, b, sems.at[n]) for n, (a, b) in enumerate(pairs)]
    for c in copies:
        c.start()
    return copies


def upward_kernel(
    vec_h, basis_h, lt_h, ct_h, mt_h,
    payload, near_msg, far_msg, lc, cl, basis, lt, ct, mt,
    vec, rows, lcs, sems,
):
    copies = fetch(sems, (vec_h, vec), (basis_h, basis), (mt_h, mt), (lt_h, lt), (ct_h, ct))
    even = lax.axis_index("rows") % 2 == 0
    own = (iota((32, 256), 1) // 64 == iota((32, 256), 0) // 8).astype(F32)
    eye = (iota((32, 32), 0) == iota((32, 32), 1)).astype(BF)
    for copy in copies[:3]:
        copy.wait()
    mtf = mt[...].astype(F32)
    mtj = [mtf[:, j, :].astype(BF) for j in range(2)]
    for c in range(32):
        x = vec[:, c * 256 : (c + 1) * 256].astype(F32)
        x = (jnp.concatenate([x] * 4, axis=0) * own).astype(BF)
        rows[c * 32 : (c + 1) * 32, 0:32] = mm_nt(x, basis[:, c * 256 : (c + 1) * 256])
    group = iota((32, 128), 1) // 16
    first = jnp.zeros((32, 128), F32)
    last = jnp.zeros((32, 128), F32)
    for v in range(8):
        x = rows[pl.ds(v, 128, stride=8), :][:, 0:32].astype(BF)
        x = mm_nt(eye, x)
        lcs[:, v * 128 : (v + 1) * 128] = x
        first = jnp.where(group == v, pltpu.roll(x, v * 16, 1) if v else x, first)
        last = jnp.where(group == v, pltpu.roll(x, v * 16 + 16, 1) if v < 7 else x, last)
    lc[...] = lcs[...].astype(BF)
    copies[3].wait()
    sums = [jnp.zeros((32, 128), F32) for _ in range(8)]
    for r in range(32):
        w = lt[r].astype(F32)
        for v in range(8):
            sums[v] = sums[v] + w * lcs[r : r + 1, v * 128 : (v + 1) * 128]
    hi, lo = halves(jnp.concatenate(sums, axis=0))
    spread = (iota((128, 128), 0) // 8 == iota((128, 128), 1) % 16).astype(BF)
    y = mm(hi, spread) + mm(lo, spread)
    c = jnp.zeros((32, 128), F32)
    for v in range(8):
        c = jnp.where(group == v, y[v * 32 : (v + 1) * 32], c)
    y = jnp.concatenate([y] * 4, axis=1)
    y = jnp.where(iota((256, 512), 0) % 32 == iota((256, 512), 1) // 16, y, 0.0).astype(BF)
    gather = (iota((8, 256), 0) == iota((8, 256), 1) // 32).astype(BF)
    y = mm(gather, y)
    half = iota((8, 512), 1) % 16 // 8
    copies[4].wait()
    pieces = []
    top = jnp.zeros((8, 32), F32)
    for j in range(2):
        m = mm(jnp.where(half == j, y, 0.0).astype(BF), ct[...]).astype(BF)
        pieces.append(m.astype(F32))
        top = top + mm(m, mtj[j])
    hi = top.astype(BF).astype(F32)
    out = jnp.concatenate(pieces + [hi, top - hi], axis=1).astype(BF)
    for z in range(8):
        payload[z] = out
    c = c.astype(BF)
    cl[...] = c
    head = vec[:, 0:256].astype(F32)
    tail = vec[:, 8192 - 256 : 8192].astype(F32)
    for ref, right in ((near_msg, even), (far_msg, jnp.logical_not(even))):
        ref[0:32, :] = jnp.where(right, last, first).astype(BF)
        ref[32:64, :] = c
        pts = jnp.where(right, tail, head)
        ref[64:80, :] = jnp.concatenate([pts[:, 0:128], pts[:, 128:256]], axis=0).astype(BF)


def compose_kernel(
    lt, basis, ct, ni_h, nc_h, li_h, ci_h, cc_h, mi_h, mcount_h, ti_h,
    wide, nidx, rel, crel, meta,
    ni, nc, li, ci, cc, mi, mcount, ti, lts, cts, turned, flat, sems,
):
    copies = fetch(
        sems, (ni_h, ni), (nc_h, nc), (li_h, li), (ci_h, ci), (cc_h, cc), (mi_h, mi), (mcount_h, mcount), (ti_h, ti)
    )
    device = lax.axis_index("rows")
    lts[...] = lt[...].reshape(1024, 128).astype(F32)
    eye = (iota((128, 128), 0) == iota((128, 128), 1)).astype(BF)
    group = iota((128, 128), 1) // 32
    for m in range(8):
        x = [lts[pl.ds(m * 4 + n, 32, stride=32), :].astype(BF) for n in range(4)]
        x = mm_nt(eye, jnp.concatenate(x, axis=0))
        for n in range(4):
            turned[pl.ds(m * 4 + n, 128, stride=32), :] = jnp.where(group == n, x, 0.0)
    low = iota((32, 128), 1) < 64
    for c in range(64):
        here = slice(c * 128, (c + 1) * 128)
        x = turned[c * 64 : (c + 1) * 64, :].astype(BF)
        r = mm(x, jnp.concatenate([basis[:, here]] * 4, axis=0))
        flat[:, here] = jnp.where(low, r[0:32], r[32:64]).astype(BF)
    cts[:, 0:32] = ct[...].astype(F32)
    for k in range(16):
        w = cts[pl.ds(k, 32, stride=16), :][:, 0:32].T.astype(BF)
        here = slice(k * 512, (k + 1) * 512)
        wide[:, here] = mm(w, flat[:, here]).astype(BF)
    for copy in copies:
        copy.wait()
    slot = iota((6, 128), 0)
    nidx[...] = jnp.where(slot < nc[...].reshape(1, 128), ni[...] - device * 128 + 4, 136)
    rel[...] = li[...] - device * 128
    x = jnp.where(iota((3, 16), 0) < cc[...].reshape(1, 16), ci[...] - device * 16, -100)
    x = jnp.concatenate([x.astype(F32), jnp.zeros((5, 16), F32)], axis=0).T
    crel[...] = jnp.concatenate([x] * 8, axis=0).astype(I32)
    t = jnp.where(iota((8, 64), 1) == device // 4, ti[...], 0)
    meta[0:8, :] = jnp.broadcast_to(jnp.sum(t, axis=1, keepdims=True), (8, 128))
    for j in range(2):
        for s in range(8):
            m = mi[j, s]
            d = m >> 1
            at = (d >> 6) * 64 + (d & 7) * 8 + ((d >> 3) & 7)
            side = jnp.where(s < mcount[j], m & 1, -1)
            meta[8 + j * 8 + s : 9 + j * 8 + s, :] = jnp.where(iota((1, 128), 1) == 0, at, side)


def field_kernel(
    nidx, rel, crel, lc, cl, near_got, far_got, mt,
    vec_h, nb_h, coup_h, ccoup_h, lt_h, basis_h, tc_h, mc_h,
    total, wide, down,
    ml, mr, vec, nb, coup, ccoup, lt, basis, tc, mc, picked, lts, fx, rows, tiles, sems,
):
    copies = fetch(
        sems, (ccoup_h, ccoup), (lt_h, lt), (vec_h, vec), (basis_h, basis),
        *[(coup_h.at[s], coup.at[s]) for s in range(8)],
    )
    later = [
        pltpu.make_async_copy(a, b, sems.at[12 + n])
        for n, (a, b) in enumerate(
            [(nb_h.at[:, :, pl.ds(n * 1024, 1024)], nb.at[n]) for n in range(8)]
            + [(tc_h, tc), (mc_h, mc)]
        )
    ]
    even = lax.axis_index("rows") % 2 == 0
    a, b = near_got[...].astype(F32), far_got[...].astype(F32)
    ml[...] = jnp.where(even, b, a).astype(BF)
    mr[...] = jnp.where(even, a, b).astype(BF)

    lcv = lc[...]
    stack = jnp.concatenate([lcv[:, v * 128 : (v + 1) * 128] for v in range(8)], axis=0)
    mine = iota((256, 128), 0) // 32 == iota((256, 128), 1) // 16
    cols = [stack]
    for ref in (ml, mr):
        edge = jnp.concatenate([ref[0:32, :].astype(F32)] * 8, axis=0)
        cols.append(jnp.where(mine, edge, 0.0).astype(BF))
    lhs = jnp.concatenate(cols, axis=1)
    where = iota((128, 128), 0)
    for s in range(8):
        at = rel[s : s + 1, :]
        onehot = jnp.concatenate(
            [
                (where == at).astype(F32),
                (where % 16 == at + 16).astype(F32),
                (where % 16 == at - 128).astype(F32),
            ],
            axis=0,
        ).astype(BF)
        picked[s] = mm(lhs, onehot)

    for copy in later[:2]:
        copy.start()

    clhs = jnp.concatenate([cl[...], ml[32:64, :], mr[32:64, :]], axis=1)
    row, lane = iota((128, 128), 0), iota((128, 128), 1)
    same = row // 16 == lane // 16
    spread = (iota((32, 512), 0) == iota((32, 512), 1) // 16).astype(BF)
    own = iota((128, 512), 0) % 16 == iota((128, 512), 1) % 16
    copies[0].wait()
    cnear = jnp.zeros((128, 32), F32)
    for s in range(3):
        at = jnp.broadcast_to(crel[:, s : s + 1], (128, 128))
        onehot = jnp.concatenate(
            [
                (same & (lane % 16 == at)).astype(F32),
                (same & (lane % 16 == at + 16)).astype(F32),
                (same & (lane % 16 == at - 16)).astype(F32),
            ],
            axis=1,
        ).astype(BF)
        x = mm_nt(onehot, clhs).astype(BF)
        x = jnp.where(own, mm(x, spread), 0.0).astype(BF)
        cnear = cnear + mm(x, ccoup[s].reshape(512, 32))
    grow = (
        (iota((128, 1024), 0) // 16 == iota((128, 1024), 1) // 128)
        & (iota((128, 1024), 0) % 16 == iota((128, 1024), 1) % 128 // 8)
    ).astype(BF)
    r = mm(cnear.T.astype(BF), grow)
    for v in range(8):
        fx[v * 32 : (v + 1) * 32, :] = r[:, v * 128 : (v + 1) * 128]

    for copy in later[2:]:
        copy.start()
    copies[1].wait()
    lts[...] = lt[...].reshape(1024, 128).astype(F32)

    def down_step(t, sums):
        q0 = t * 4
        for n in range(4):
            w = lts[pl.ds(q0 + n, 32, stride=32), :]
            sums = tuple(
                sums[v] + w * fx[pl.ds(v * 32 + q0 + n, 1), :] for v in range(8)
            )
        return sums

    sums = tuple(jnp.zeros((32, 128), F32) for _ in range(8))
    sums = lax.fori_loop(0, 8, down_step, sums)

    low = iota((8, 128), 1) < 64

    def put(x, at):
        y = pltpu.roll(x, 64, 1)
        tiles[at] = jnp.where(low, x, y)
        tiles[at + 1] = jnp.where(low, y, x)

    copies[2].wait()
    for p in range(64):
        put(vec[:, p * 128 : (p + 1) * 128].astype(F32), 4 + 2 * p)
    for ref, at in ((ml, 0), (mr, 132)):
        pts = ref[64:80, :].astype(F32)
        put(pts[0:8], at)
        put(pts[8:16], at + 2)
    tiles[136] = jnp.zeros((8, 128), F32)

    for t in range(32):
        s, p0 = t // 4, t % 4 * 8
        if t % 4 == 0:
            copies[4 + s].wait()
            later[s].wait()
        for p in range(p0, p0 + 8):
            w = coup[s, p].astype(F32)
            sums = [sums[v] + w * picked[s, v * 32 + p : v * 32 + p + 1, :] for v in range(8)]
        parts = []
        for l in range(4):
            i = t * 4 + l
            parts.append(
                jnp.concatenate(
                    [
                        jnp.where(low, tiles[nidx[2 * n, i]], tiles[nidx[2 * n + 1, i]])
                        for n in range(3)
                    ],
                    axis=1,
                )
            )
        x = jnp.concatenate(parts, axis=0).astype(BF)
        a, c = t * 256, t % 4 * 256
        r = mm(x, nb[t // 4, :, :, c : c + 256].reshape(384, 256))
        total[:, a : a + 128] = jnp.where(low, r[0:8, 0:128], r[8:16, 0:128])
        total[:, a + 128 : a + 256] = jnp.where(low, r[16:24, 128:256], r[24:32, 128:256])

    eye = (iota((128, 128), 0) == iota((128, 128), 1)).astype(BF)
    for v in range(8):
        rows[pl.ds(v, 128, stride=8), 0:32] = mm_nt(eye, sums[v].astype(BF))
    copies[3].wait()
    for c in range(64):
        here = slice(c * 128, (c + 1) * 128)
        r = mm(rows[c * 16 : (c + 1) * 16, 0:32].astype(BF), basis[:, here])
        total[:, here] = total[:, here] + jnp.where(low, r[0:8], r[8:16])

    device = lax.axis_index("rows")
    pick = (iota((8, 64), 1) == device // 4).astype(BF)
    keep = iota((32, 1024), 0) == iota((32, 1024), 1) // 32
    fold = (iota((1024, 32), 0) % 32 == iota((1024, 32), 1)).astype(BF)
    later[8].wait()
    later[9].wait()
    none = jnp.zeros((32, 32), F32)
    for s in range(8):
        x = mm_nt(pick, tc[s].reshape(1024, 64))
        x = jnp.where(keep, jnp.broadcast_to(x[0:1], (32, 1024)), 0.0).astype(BF)
        top = jnp.concatenate([none, none, mm(x, fold), none], axis=1).astype(BF)
        x = mc[s].astype(F32)
        middle = jnp.concatenate([x[:, 0, :], x[:, 1, :], none, none], axis=1).astype(BF)
        for n, x in enumerate((middle, middle, top, top)):
            wide[s * 128 + n * 32 : s * 128 + n * 32 + 32, :] = x
    mtf = mt[...].astype(F32)
    for j in range(2):
        down[j] = mtf[:, j, :].T.astype(BF)


def spread_kernel(got, meta, near_got, far_got, out):
    x = got[...]
    for n in range(32):
        out[n] = x


def tail_kernel(meta, got, wm, down, total, wide, out):
    lane = iota((8, 128), 1) // 32

    def block(d):
        return got[(d >> 6) * 64 + (d & 7) * 8 + ((d >> 3) & 7)].astype(F32)

    rows = [[], [], []]
    for s in range(8):
        for j in range(2):
            x = got[meta[8 + j * 8 + s, 0]].astype(F32)
            rows[j].append(jnp.where(lane == meta[8 + j * 8 + s, 1], x, 0.0))
        t = meta[s, 0]
        x = (block(4 * t) + block(4 * t + 1)) + (block(4 * t + 2) + block(4 * t + 3))
        rows[2].append(jnp.where(lane >= 2, x, 0.0))
    x = jnp.concatenate([jnp.concatenate(r, axis=1) for r in rows], axis=0).astype(BF)
    x = mm(x, wm[...])
    field = x[16:24, 64:96].astype(BF)
    for j in range(2):
        f = x[j * 8 : (j + 1) * 8, j * 32 : (j + 1) * 32] + mm(field, down[j])
        f = f.astype(BF)
        here = slice(j * 4096, (j + 1) * 4096)
        out[:, here] = (total[:, here] + mm(f, wide[:, here])).astype(BF)


def vm():
    return pl.BlockSpec(memory_space=pltpu.VMEM)


def sm():
    return pl.BlockSpec(memory_space=pltpu.SMEM)


def hbm():
    return pl.BlockSpec(memory_space=pltpu.HBM)


def far_away(x):
    return pltpu.with_memory_space_constraint(x, pltpu.HBM)


def params(mib):
    return pltpu.CompilerParams(vmem_limit_bytes=mib * MIB)


def cost(flops, nbytes):
    return pl.CostEstimate(flops=flops, bytes_accessed=nbytes, transcendentals=0)


def body(
    vectors,
    basis_leaf,
    near_block,
    near_index,
    near_count,
    leaf_trans,
    leaf_coupling,
    leaf_index,
    cluster_trans,
    cluster_coupling,
    cluster_index,
    cluster_count,
    middle_trans,
    middle_coupling,
    middle_index,
    middle_count,
    top_coupling,
    top_index,
):
    S = jax.ShapeDtypeStruct
    V = pltpu.VMEM
    DMA = pltpu.SemaphoreType.DMA
    ct_rows = jnp.transpose(cluster_trans, (0, 2, 1)).reshape(512, 32)
    mt_rows = jnp.transpose(middle_trans, (0, 2, 1))
    payload, near_msg, far_msg, lc, cl, basis, lt, ct, mt = pl.pallas_call(
        upward_kernel,
        out_shape=(
            S((8, 8, 128), BF), S((80, 128), BF), S((80, 128), BF), S((32, 1024), BF), S((32, 128), BF),
            S((32, 8192), BF), S((32, 32, 128), BF), S((512, 32), BF), S((32, 2, 32), BF),
        ),
        in_specs=[hbm()] * 5,
        out_specs=(vm(),) * 9,
        scratch_shapes=[V((8, 8192), BF), V((1024, 128), F32), V((32, 1024), F32), DMA((5,))],
        compiler_params=params(16),
        cost_estimate=cost(10**8, 1 * MIB),
        name="upward",
    )(*map(far_away, (vectors, basis_leaf, leaf_trans, ct_rows, mt_rows)))

    def device_id(x, z, y, c):
        return ((x * 8 + z) * 4 + y) * 2 + c

    rest = [(x, y, c) for x in range(4) for y in range(4) for c in range(2)]
    along_z = [[device_id(x, z, y, c) for z in range(8)] for x, y, c in rest]
    across = [[device_id(x, z, y, c) for x, y, c in rest] for z in range(8)]
    got = lax.all_to_all(payload, "rows", 0, 0, axis_index_groups=along_z, tiled=True)

    far_got = lax.ppermute(
        far_msg, "rows", [(i, ((i + 1) ^ 1) - 1) for i in range(1, 255)]
    )
    near_got = lax.ppermute(near_msg, "rows", [(i, i ^ 1) for i in range(256)])

    bases, nidx, rel, crel, meta = pl.pallas_call(
        compose_kernel,
        out_shape=(
            S((32, 8192), BF), S((6, 128), I32), S((8, 128), I32), S((128, 8), I32), S((24, 128), I32),
        ),
        in_specs=[vm()] * 3 + [hbm()] * 8,
        out_specs=(vm(),) * 5,
        scratch_shapes=[
            V((6, 128), I32), V((128,), I32), V((8, 128), I32), V((3, 16), I32), V((16,), I32),
            pltpu.SMEM((2, 8), I32), pltpu.SMEM((2,), I32), V((8, 64), I32),
            V((1024, 128), F32), V((512, 128), F32), V((4096, 128), F32), V((32, 8192), BF),
            DMA((8,)),
        ],
        compiler_params=params(16),
        cost_estimate=cost(10**9, 2 * MIB),
        name="compose",
    )(
        lt, basis, ct,
        *map(
            far_away,
            (
                near_index, near_count, leaf_index, cluster_index, cluster_count,
                jnp.transpose(middle_index), middle_count, top_index,
            ),
        ),
    )

    got = pl.pallas_call(
        spread_kernel,
        out_shape=S((32, 64, 128), BF),
        in_specs=[vm()] * 4,
        out_specs=vm(),
        compiler_params=params(16),
        cost_estimate=cost(10**5, MIB // 2),
        name="spread",
    )(got.reshape(64, 128), meta, near_got, far_got)
    got = lax.all_to_all(got, "rows", 0, 0, axis_index_groups=across, tiled=True)
    got = got.reshape(256, 8, 128)

    total, tables, down = pl.pallas_call(
        field_kernel,
        out_shape=(S((8, 8192), F32), S((1024, 128), BF), S((2, 32, 32), BF)),
        in_specs=[sm()] + [vm()] * 7 + [hbm()] * 8,
        out_specs=(vm(),) * 3,
        scratch_shapes=[
            V((80, 128), BF), V((80, 128), BF), V((8, 8192), BF), V((8, 6, 64, 1024), BF),
            V((8, 32, 32, 128), BF), V((3, 32, 16, 32), BF), V((32, 32, 128), BF), V((32, 8192), BF),
            V((8, 32, 32, 64), BF), V((8, 32, 2, 32), BF),
            V((8, 256, 128), F32), V((1024, 128), F32), V((256, 128), F32), V((1024, 128), F32),
            V((137, 8, 128), F32), DMA((22,)),
        ],
        compiler_params=params(32),
        cost_estimate=cost(2 * 10**9, 12 * MIB),
        name="field",
    )(
        nidx, rel, crel, lc, cl, near_got, far_got, mt,
        *map(
            far_away,
            (
                vectors, near_block, leaf_coupling, jnp.transpose(cluster_coupling, (0, 1, 3, 2)),
                leaf_trans, basis_leaf, top_coupling, jnp.transpose(middle_coupling, (0, 1, 3, 2)),
            ),
        ),
    )

    return pl.pallas_call(
        tail_kernel,
        out_shape=S((8, 8192), BF),
        in_specs=[sm()] + [vm()] * 5,
        out_specs=vm(),
        compiler_params=params(16),
        cost_estimate=cost(10**8, 2 * MIB),
        name="tail",
    )(meta, got, tables, down, total, bases)


def solution(mesh):
    in_specs = (
        P(None, "rows"),
        P(None, "rows"),
        P(None, None, "rows"),
        P(None, "rows"),
        P("rows"),
        P(None, None, "rows"),
        P(None, None, None, "rows"),
        P(None, "rows"),
        P(None, None, "rows"),
        P(None, None, None, "rows"),
        P(None, "rows"),
        P("rows"),
        P(None, None, "rows"),
        P(None, None, None, "rows"),
        P(None, "rows"),
        P("rows"),
        P(),
        P(),
    )
    out_specs = P(None, "rows")
    return jax.shard_map(body, mesh=mesh, in_specs=in_specs, out_specs=out_specs, check_vma=False)
```

time: 355 us -> 43.4 us (0.12); the launches traced: 349 us -> 43.1 us
  blocking collectives: 149 us -> 0 us
  local copies, waits for them, and re-layouts: 105 us -> 0 us
  matrix products: 57.7 us -> 0 us
  Pallas kernels: 0 us -> 19.9 us
  other arithmetic: 7.36 us -> 0 us
  starting transfers between devices: 29.2 us -> 22.2 us
    all_gather x1 -> x0, blocking collectives: 75.3 us -> none  [body(): shard_coef = lax.all_gather(coef_middle, 'rows', axis=2, tiled=True)]
    psum x1 -> x0, blocking collectives: 74.2 us -> none  [body(): coef_top = lax.psum(slot_table, 'rows').astype(jnp.bfloat16)]
    dot_general x16 -> x0, matrix products: 57.7 us -> none  [the longest x1 30.1 us: body(): jnp.einsum('svib,sbia->via', picked_near, blocks, preferred_element_type=...]
    unnamed x50 -> x0, local copies, waits for them, and re-layouts: 38.4 us -> none
    ppermute x6 -> x2, starting transfers between devices: 29.2 us -> 4.05 us  [the longest x1 3.09 us: body(): lax.ppermute(far_msg, 'rows', [(i, (i + 1 ^ 1) - 1) for i in range(1, 255)])]
    reshape x5 -> x0, local copies, waits for them, and re-layouts: 24.6 us -> none  [the longest x1 17.9 us: body(): blocks = near_block.reshape(near_slots, LEAF, leaves, LEAF)]
    pallas_call x0 -> x5, Pallas kernels: none -> 19.9 us  [the longest x1 10.7 us: body(): pl.pallas_call(field_kernel, out_shape=(S((8, 8192), F32), S((1024, 128),...]
    all_to_all x0 -> x2, starting transfers between devices: none -> 18.1 us  [the longest x1 9.12 us: body(): lax.all_to_all(got, 'rows', 0, 0, axis_index_groups=across, tiled=True)]
  transfers between devices with their start and end apart: 6 -> 4, of which waited for: 0 -> 1; matrix products, arithmetic and copies ran while one was open for 36% -> 0% of each run, Pallas kernels for 0% -> 31%
where the time goes in v1:
time: 43.4 us; the launch traced here: 43.1 us
  starting transfers between devices  22.2 us (51%)
  Pallas kernels  19.9 us (46%)
  waiting for transfers between devices  0.92 us (2%)
    pallas_call x1, Pallas kernels, body(): pl.pallas_call(field_kernel, out_shape=(S((8, 8192), F32), S((1024, 128),...  10.7 us
    all_to_all x1, starting transfers between devices, body(): lax.all_to_all(got, 'rows', 0, 0, axis_index_groups=across, tiled=True)  9.12 us
    all_to_all x1, starting transfers between devices, body(): lax.all_to_all(payload, 'rows', 0, 0, axis_index_groups=along_z, tiled=True)  9.02 us
    pallas_call x1, Pallas kernels, body(): pl.pallas_call(upward_kernel, out_shape=(S((8, 8, 128), BF), S((80, 128),...  3.39 us
    ppermute x1, starting transfers between devices, body(): lax.ppermute(far_msg, 'rows', [(i, (i + 1 ^ 1) - 1) for i in range(1, 255)])  3.09 us
    pallas_call x1, Pallas kernels, body(): pl.pallas_call(compose_kernel, out_shape=(S((32, 8192), BF), S((6, 128),...  2.59 us
    pallas_call x1, Pallas kernels, body(): pl.pallas_call(tail_kernel, out_shape=S((8, 8192), BF), in_specs=[sm()] +...  2.27 us
    ppermute x1, starting transfers between devices, body(): near_got = lax.ppermute(near_msg, 'rows', [(i, i ^ 1) for i in range(256)])  0.96 us
  transfers between devices with their start and end apart: 4, of which 1 were waited for; matrix products, arithmetic and copies ran while one was open for 0% of the time, Pallas kernels for 31%

profile of v1, /device:TPU:1, one launch (start us, length us, event | category | flops | bytes accessed | tf_op | source)
XLA Modules:
  0.0 43.1 jit_solution(6646204819024577921)
XLA Ops:
  0.0 3.4 %upward.1 = (bf16[8,8,128]{2,1,0:T(8,128)(2,1)}, bf16[80,128]{1,0:T(8,128)(2,1)S(1)}, bf16[80,128]{1,0:T(8,128)(2,1)S(1)}, bf16[32,1024]{1,0:T(8,128)(2,1)S(1)},...) custom-call(bf16[8,8192]{1,0:T(8,128)(2,1)} %vec_h.3, ...), custom_call_target="tpu_custom_call" | custom-call | flops 100000000 | bytes 1048576 | tf_op jit(solution)/shard_map/upward/pallas_call | solution.py:393
  3.4 9.0 %all-to-all-start = ((bf16[8,8,128]{2,1,0:T(8,128)(2,1)}), bf16[8,8,128]{2,1,0:T(8,128)(2,1)S(1)}, u32[]{:S(2)}, u32[]{:S(2)}) async-start(bf16[8,8,128]{2,1,0:T(8,128)(2,1)} %get-tuple-element.26), calls=%async_computation | async-start | bytes 32768 | tf_op jit(solution)/shard_map/all_to_all | solution.py:413
  12.4 1.0 %collective-permute-start = (bf16[80,128]{1,0:T(8,128)(2,1)S(1)}, bf16[80,128]{1,0:T(8,128)(2,1)S(1)}, u32[]{:S(2)}, u32[]{:S(2)}) collective-permute-start(bf16[80,128]{1,0:T(8,128)(2,1)S(1)} %get-tuple-element.27), channel_id=1, source_target_pairs={{0,1},{1,0},{2,3},{3,2},{4,5},{5,4},{6,7},{7,6},{8,9},{9,8},{10,11... | collective-permute-start | bytes 61448 | tf_op jit(solution)/shard_map/ppermute | solution.py:418
  13.4 3.1 %collective-permute-start.1 = (bf16[80,128]{1,0:T(8,128)(2,1)S(1)}, bf16[80,128]{1,0:T(8,128)(2,1)S(1)}, u32[]{:S(2)}, u32[]{:S(2)}) collective-permute-start(bf16[80,128]{1,0:T(8,128)(2,1)S(1)} %get-tuple-element.28), channel_id=1, source_target_pairs={{1,2},{2,1},{3,4},{4,3},{5,6},{6,5},{7,8},{8,7},{9,10},{10,9},{11,... | collective-permute-start | bytes 61448 | tf_op jit(solution)/shard_map/ppermute | solution.py:415
  16.5 2.6 %compose.1 = (bf16[32,8192]{1,0:T(8,128)(2,1)S(1)}, s32[6,128]{1,0:T(8,128)S(1)}, s32[8,128]{1,0:T(8,128)S(1)}, s32[128,8]{1,0:T(8,128)S(1)}, s32[24,128]{1,0:T(8,128)S(1)}) custom-call(bf16[32,32,128]{2,1,0:T(8,128)(2,1)S(1)} %get-tuple-element.22.lt, bf16[32,8192]{1,0:T(8,128)(2,1)S(1)} %get-tuple-element.23.basis, ...), custom_call_target="tpu_custom_call" | custom-call | flops 1000000000 | bytes 2097152 | tf_op jit(solution)/shard_map/compose/pallas_call | solution.py:420
  19.1 0.0 collective-permute-done.near_got
  19.1 0.0 collective-permute-done.1.far_got
  19.1 0.0 all-to-all-done
  19.1 0.9 %spread.1 = bf16[32,64,128]{2,1,0:T(8,128)(2,1)} custom-call(bf16[64,128]{1,0:T(8,128)(2,1)S(1)} %bitcast.10, s32[24,128]{1,0:T(8,128)S(1)} %get-tuple-element.25.meta, bf16[80,128]{1,0:T(8,128)(2,1)S(1)} %collective-permute-done.near_got, bf16[80,128]{1,0:T(8,128)(2,1)S(1)} %collective-permute-done.1.far_got), custom_call_target="tpu_custom_call" | custom-call | flops 100000 | bytes 524288 | tf_op jit(solution)/shard_map/spread/pallas_call | solution.py:447
  20.0 9.1 %all-to-all-start.1 = ((bf16[32,64,128]{2,1,0:T(8,128)(2,1)}), bf16[32,64,128]{2,1,0:T(8,128)(2,1)S(1)}, u32[]{:S(2)}, u32[]{:S(2)}) async-start(bf16[32,64,128]{2,1,0:T(8,128)(2,1)} %spread.1), calls=%async_computation.1 | async-start | bytes 1048576 | tf_op jit(solution)/shard_map/all_to_all | solution.py:456
  29.2 10.7 %field.1 = (f32[8,8192]{1,0:T(8,128)S(1)}, bf16[1024,128]{1,0:T(8,128)(2,1)S(1)}, bf16[2,32,32]{2,1,0:T(8,128)(2,1)S(1)}) custom-call(s32[6,128]{1,0:T(8,128)S(1)} %get-tuple-element.29.nidx, s32[8,128]{1,0:T(8,128)S(1)} %get-tuple-element.30.rel, s32[128,8]{1,0:T(8,128)S(1)} %get-tuple-element.31.crel, bf16[32,1024]{1,0:T(8,128)(2,1)S(1)} %get-tuple-element.32.lc, ...), custom_call_target="tpu_custom_call" | custom-call | flops 2000000000 | bytes 12582912 | tf_op jit(solution)/shard_map/field/pallas_call | solution.py:459
  39.9 0.9 %all-to-all-done.1 = bf16[32,64,128]{2,1,0:T(8,128)(2,1)S(1)} async-done(((bf16[32,64,128]{2,1,0:T(8,128)(2,1)}), bf16[32,64,128]{2,1,0:T(8,128)(2,1)S(1)}, u32[]{:S(2)}, u32[]{:S(2)}) %all-to-all-start.1) | async-done | bytes 524320 | tf_op jit(solution)/shard_map/all_to_all | solution.py:456
  40.8 2.3 %tail.1 = bf16[8,8192]{1,0:T(8,128)(2,1)} custom-call(s32[24,128]{1,0:T(8,128)S(1)} %get-tuple-element.25.meta, bf16[256,8,128]{2,1,0:T(8,128)(2,1)S(1)} %bitcast.9, bf16[1024,128]{1,0:T(8,128)(2,1)S(1)} %get-tuple-element.35.wm, bf16[2,32,32]{2,1,0:T(8,128)(2,1)S(1)} %get-tuple-element.36.down, f32[8,8192]{1,0:T(8,128)S(1)} %get-tuple-element.37.total, ...), custom_call_target="tpu_custom_call" | custom-call | flops 100000000 | bytes 2097152 | tf_op jit(solution)/shard_map/tail/pallas_call | solution.py:485
Async XLA Ops:
  3.4 15.7 %all-to-all-start = ((bf16[8,8,128]{2,1,0:T(8,128)(2,1)}), bf16[8,8,128]{2,1,0:T(8,128)(2,1)S(1)}, u32[]{:S(2)}, u32[]{:S(2)}) async-start(bf16[8,8,128]{2,1,0:T(8,128)(2,1)} %get-tuple-element.26), calls=%async_computation | async-start | bytes 32768 | tf_op jit(solution)/shard_map/all_to_all | solution.py:413
  12.4 6.7 %collective-permute-start = (bf16[80,128]{1,0:T(8,128)(2,1)S(1)}, bf16[80,128]{1,0:T(8,128)(2,1)S(1)}, u32[]{:S(2)}, u32[]{:S(2)}) collective-permute-start(bf16[80,128]{1,0:T(8,128)(2,1)S(1)} %get-tuple-element.27), channel_id=1, source_target_pairs={{0,1},{1,0},{2,3},{3,2},{4,5},{5,4},{6,7},{7,6},{8,9},{9,8},{10,11... | collective-permute-start | bytes 61448 | tf_op jit(solution)/shard_map/ppermute | solution.py:418
  13.4 5.7 %collective-permute-start.1 = (bf16[80,128]{1,0:T(8,128)(2,1)S(1)}, bf16[80,128]{1,0:T(8,128)(2,1)S(1)}, u32[]{:S(2)}, u32[]{:S(2)}) collective-permute-start(bf16[80,128]{1,0:T(8,128)(2,1)S(1)} %get-tuple-element.28), channel_id=1, source_target_pairs={{1,2},{2,1},{3,4},{4,3},{5,6},{6,5},{7,8},{8,7},{9,10},{10,9},{11,... | collective-permute-start | bytes 61448 | tf_op jit(solution)/shard_map/ppermute | solution.py:415
  20.0 20.7 %all-to-all-start.1 = ((bf16[32,64,128]{2,1,0:T(8,128)(2,1)}), bf16[32,64,128]{2,1,0:T(8,128)(2,1)S(1)}, u32[]{:S(2)}, u32[]{:S(2)}) async-start(bf16[32,64,128]{2,1,0:T(8,128)(2,1)} %spread.1), calls=%async_computation.1 | async-start | bytes 1048576 | tf_op jit(solution)/shard_map/all_to_all | solution.py:456

commit v2 on v1

--- a/solution.py
+++ b/solution.py
@@ -89,7 +89,7 @@
         top = top + mm(m, mtj[j])
     hi = top.astype(BF).astype(F32)
     out = jnp.concatenate(pieces + [hi, top - hi], axis=1).astype(BF)
-    for z in range(8):
+    for z in range(16):
         payload[z] = out
     c = c.astype(BF)
     cl[...] = c
@@ -104,8 +104,8 @@
 
 def compose_kernel(
     lt, basis, ct, ni_h, nc_h, li_h, ci_h, cc_h, mi_h, mcount_h, ti_h,
-    wide, nidx, rel, crel, meta,
-    ni, nc, li, ci, cc, mi, mcount, ti, lts, cts, turned, flat, sems,
+    wide, flat, nidx, rel, crel, meta,
+    ni, nc, li, ci, cc, mi, mcount, ti, lts, cts, turned, sems,
 ):
     copies = fetch(
         sems, (ni_h, ni), (nc_h, nc), (li_h, li), (ci_h, ci), (cc_h, cc), (mi_h, mi), (mcount_h, mcount), (ti_h, ti)
@@ -144,28 +144,30 @@
         for s in range(8):
             m = mi[j, s]
             d = m >> 1
-            at = (d >> 6) * 64 + (d & 7) * 8 + ((d >> 3) & 7)
+            at = (d >> 6) * 64 + ((d >> 1) & 3) * 16 + ((d >> 3) & 7) * 2 + (d & 1)
             side = jnp.where(s < mcount[j], m & 1, -1)
             meta[8 + j * 8 + s : 9 + j * 8 + s, :] = jnp.where(iota((1, 128), 1) == 0, at, side)
 
 
 def field_kernel(
-    nidx, rel, crel, lc, cl, near_got, far_got, mt,
-    vec_h, nb_h, coup_h, ccoup_h, lt_h, basis_h, tc_h, mc_h,
+    nidx, rel, crel, lc, cl, near_got, far_got, mt, flat,
+    vec_h, nb_h, coup_h, ccoup_h, basis_h, tc_h, mc_h,
     total, wide, down,
-    ml, mr, vec, nb, coup, ccoup, lt, basis, tc, mc, picked, lts, fx, rows, tiles, sems,
+    ml, mr, vec, nb, coup, ccoup, basis, tc, mc, picked, partial, rows, tiles, sems,
 ):
-    copies = fetch(
-        sems, (ccoup_h, ccoup), (lt_h, lt), (vec_h, vec), (basis_h, basis),
-        *[(coup_h.at[s], coup.at[s]) for s in range(8)],
-    )
-    later = [
-        pltpu.make_async_copy(a, b, sems.at[12 + n])
-        for n, (a, b) in enumerate(
-            [(nb_h.at[:, :, pl.ds(n * 1024, 1024)], nb.at[n]) for n in range(8)]
-            + [(tc_h, tc), (mc_h, mc)]
-        )
-    ]
+    order = [(vec_h, vec), (ccoup_h, ccoup), (mc_h, mc)]
+    for s in range(8):
+        order.append((coup_h.at[s], coup.at[s]))
+        order.append((nb_h.at[:, :, pl.ds(s * 1024, 1024)], nb.at[s]))
+        order.append((tc_h.at[s], tc.at[s]))
+    order.append((basis_h, basis))
+    copies = [pltpu.make_async_copy(a, b, sems.at[n]) for n, (a, b) in enumerate(order)]
+
+    def start(first, last):
+        for copy in copies[first:last]:
+            copy.start()
+
+    start(0, 9)
     even = lax.axis_index("rows") % 2 == 0
     a, b = near_got[...].astype(F32), far_got[...].astype(F32)
     ml[...] = jnp.where(even, b, a).astype(BF)
@@ -173,73 +175,22 @@
 
     lcv = lc[...]
     stack = jnp.concatenate([lcv[:, v * 128 : (v + 1) * 128] for v in range(8)], axis=0)
-    mine = iota((256, 128), 0) // 32 == iota((256, 128), 1) // 16
-    cols = [stack]
-    for ref in (ml, mr):
-        edge = jnp.concatenate([ref[0:32, :].astype(F32)] * 8, axis=0)
-        cols.append(jnp.where(mine, edge, 0.0).astype(BF))
-    lhs = jnp.concatenate(cols, axis=1)
-    where = iota((128, 128), 0)
-    for s in range(8):
-        at = rel[s : s + 1, :]
-        onehot = jnp.concatenate(
-            [
-                (where == at).astype(F32),
-                (where % 16 == at + 16).astype(F32),
-                (where % 16 == at - 128).astype(F32),
-            ],
-            axis=0,
-        ).astype(BF)
-        picked[s] = mm(lhs, onehot)
-
-    for copy in later[:2]:
-        copy.start()
-
-    clhs = jnp.concatenate([cl[...], ml[32:64, :], mr[32:64, :]], axis=1)
-    row, lane = iota((128, 128), 0), iota((128, 128), 1)
-    same = row // 16 == lane // 16
-    spread = (iota((32, 512), 0) == iota((32, 512), 1) // 16).astype(BF)
-    own = iota((128, 512), 0) % 16 == iota((128, 512), 1) % 16
-    copies[0].wait()
-    cnear = jnp.zeros((128, 32), F32)
-    for s in range(3):
-        at = jnp.broadcast_to(crel[:, s : s + 1], (128, 128))
-        onehot = jnp.concatenate(
-            [
-                (same & (lane % 16 == at)).astype(F32),
-                (same & (lane % 16 == at + 16)).astype(F32),
-                (same & (lane % 16 == at - 16)).astype(F32),
-            ],
-            axis=1,
-        ).astype(BF)
-        x = mm_nt(onehot, clhs).astype(BF)
-        x = jnp.where(own, mm(x, spread), 0.0).astype(BF)
-        cnear = cnear + mm(x, ccoup[s].reshape(512, 32))
-    grow = (
-        (iota((128, 1024), 0) // 16 == iota((128, 1024), 1) // 128)
-        & (iota((128, 1024), 0) % 16 == iota((128, 1024), 1) % 128 // 8)
-    ).astype(BF)
-    r = mm(cnear.T.astype(BF), grow)
+    lane = iota((32, 128), 1)
+    left, right = ml[0:32, :].astype(F32), mr[0:32, :].astype(F32)
+    edge = []
     for v in range(8):
-        fx[v * 32 : (v + 1) * 32, :] = r[:, v * 128 : (v + 1) * 128]
-
-    for copy in later[2:]:
-        copy.start()
-    copies[1].wait()
-    lts[...] = lt[...].reshape(1024, 128).astype(F32)
-
-    def down_step(t, sums):
-        q0 = t * 4
-        for n in range(4):
-            w = lts[pl.ds(q0 + n, 32, stride=32), :]
-            sums = tuple(
-                sums[v] + w * fx[pl.ds(v * 32 + q0 + n, 1), :] for v in range(8)
-            )
-        return sums
-
-    sums = tuple(jnp.zeros((32, 128), F32) for _ in range(8))
-    sums = lax.fori_loop(0, 8, down_step, sums)
-
+        a = pltpu.roll(left, 128 - v * 16, 1) if v else left
+        b = pltpu.roll(right, (144 - v * 16) % 128, 1) if v != 1 else right
+        edge.append(jnp.where(lane < 16, a, b))
+    edge = jnp.concatenate(edge, axis=0)[:, 0:32].astype(BF)
+    lhs = jnp.concatenate([stack, edge], axis=1)
+    where = iota((160, 128), 0)
+    where = where - jnp.where(where < 128, 0, jnp.where(where < 144, 144, 16))
+    for s in range(0, 8, 2):
+        onehot = [(where == rel[n : n + 1, :]).astype(F32) for n in (s, s + 1)]
+        x = mm(lhs, jnp.concatenate(onehot, axis=1).astype(BF))
+        picked[s] = x[:, 0:128]
+        picked[s + 1] = x[:, 128:256]
     low = iota((8, 128), 1) < 64
 
     def put(x, at):
@@ -247,7 +198,7 @@
         tiles[at] = jnp.where(low, x, y)
         tiles[at + 1] = jnp.where(low, y, x)
 
-    copies[2].wait()
+    copies[0].wait()
     for p in range(64):
         put(vec[:, p * 128 : (p + 1) * 128].astype(F32), 4 + 2 * p)
     for ref, at in ((ml, 0), (mr, 132)):
@@ -256,11 +207,58 @@
         put(pts[8:16], at + 2)
     tiles[136] = jnp.zeros((8, 128), F32)
 
+    row, lane = iota((128, 128), 0), iota((128, 128), 1)
+    same = row // 16 == lane // 16
+    spread = (iota((32, 512), 0) == iota((32, 512), 1) // 16).astype(BF)
+    own = iota((128, 512), 0) % 16 == iota((128, 512), 1) % 16
+    partners = []
+
+    def cluster_pick():
+        clhs = jnp.concatenate([cl[...], ml[32:64, :], mr[32:64, :]], axis=1)
+        for s in range(3):
+            at = jnp.broadcast_to(crel[:, s : s + 1], (128, 128))
+            onehot = [same & (lane % 16 == at + n) for n in (0, 16, -16)]
+            onehot = jnp.concatenate([o.astype(F32) for o in onehot], axis=1).astype(BF)
+            partners.append(mm_nt(onehot, clhs).astype(BF))
+
+    def cluster_couple():
+        copies[1].wait()
+        field = jnp.zeros((128, 32), F32)
+        for s in range(3):
+            x = jnp.where(own, mm(partners[s], spread), 0.0).astype(BF)
+            field = field + mm(x, ccoup[s].reshape(512, 32))
+        partners.append(field)
+
+    def cluster_store():
+        partial[:, 0:32] = partners[3]
+
+    device = lax.axis_index("rows")
+    pick = (iota((8, 64), 1) == device // 4).astype(BF)
+    keep = iota((32, 1024), 0) == iota((32, 1024), 1) // 32
+    fold = (iota((1024, 32), 0) % 32 == iota((1024, 32), 1)).astype(BF)
+    none = jnp.zeros((32, 32), F32)
+
+    def top_table(s):
+        x = mm_nt(pick, tc[s].reshape(1024, 64))
+        x = jnp.where(keep, jnp.broadcast_to(x[0:1], (32, 1024)), 0.0).astype(BF)
+        top = jnp.concatenate([none, none, mm(x, fold), none], axis=1).astype(BF)
+        wide[s * 128 + 64 : s * 128 + 96, :] = top
+        wide[s * 128 + 96 : s * 128 + 128, :] = top
+
+    def middle_table(s):
+        x = mc[s].astype(F32)
+        middle = jnp.concatenate([x[:, 0, :], x[:, 1, :], none, none], axis=1).astype(BF)
+        wide[s * 128 : s * 128 + 32, :] = middle
+        wide[s * 128 + 32 : s * 128 + 64, :] = middle
+
+    sums = [jnp.zeros((32, 128), F32) for _ in range(8)]
     for t in range(32):
         s, p0 = t // 4, t % 4 * 8
         if t % 4 == 0:
-            copies[4 + s].wait()
-            later[s].wait()
+            for copy in copies[3 + s * 3 : 6 + s * 3]:
+                copy.wait()
+            if s < 7:
+                start(9 + s * 3, min(12 + s * 3, 28))
         for p in range(p0, p0 + 8):
             w = coup[s, p].astype(F32)
             sums = [sums[v] + w * picked[s, v * 32 + p : v * 32 + p + 1, :] for v in range(8)]
@@ -278,42 +276,41 @@
             )
         x = jnp.concatenate(parts, axis=0).astype(BF)
         a, c = t * 256, t % 4 * 256
-        r = mm(x, nb[t // 4, :, :, c : c + 256].reshape(384, 256))
+        r = mm(x, nb[s, :, :, c : c + 256].reshape(384, 256))
         total[:, a : a + 128] = jnp.where(low, r[0:8, 0:128], r[8:16, 0:128])
         total[:, a + 128 : a + 256] = jnp.where(low, r[16:24, 128:256], r[24:32, 128:256])
-
+        if t % 4 == 1:
+            top_table(s)
+        if t == 2:
+            cluster_pick()
+        if t == 6:
+            cluster_couple()
+        if t == 10:
+            cluster_store()
+            copies[2].wait()
+        if t >= 11 and t % 2 == 0 and t < 27:
+            middle_table((t - 12) // 2)
+
+    mtf = mt[...].astype(F32)
+    for j in range(2):
+        down[j] = mtf[:, j, :].T.astype(BF)
     eye = (iota((128, 128), 0) == iota((128, 128), 1)).astype(BF)
     for v in range(8):
         rows[pl.ds(v, 128, stride=8), 0:32] = mm_nt(eye, sums[v].astype(BF))
-    copies[3].wait()
+    copies[27].wait()
+    for k in range(16):
+        x = partial[pl.ds(k, 8, stride=16), :][:, 0:32].astype(BF)
+        here = slice(k * 512, (k + 1) * 512)
+        total[:, here] = total[:, here] + mm(x, flat[:, here])
     for c in range(64):
         here = slice(c * 128, (c + 1) * 128)
         r = mm(rows[c * 16 : (c + 1) * 16, 0:32].astype(BF), basis[:, here])
         total[:, here] = total[:, here] + jnp.where(low, r[0:8], r[8:16])
 
-    device = lax.axis_index("rows")
-    pick = (iota((8, 64), 1) == device // 4).astype(BF)
-    keep = iota((32, 1024), 0) == iota((32, 1024), 1) // 32
-    fold = (iota((1024, 32), 0) % 32 == iota((1024, 32), 1)).astype(BF)
-    later[8].wait()
-    later[9].wait()
-    none = jnp.zeros((32, 32), F32)
-    for s in range(8):
-        x = mm_nt(pick, tc[s].reshape(1024, 64))
-        x = jnp.where(keep, jnp.broadcast_to(x[0:1], (32, 1024)), 0.0).astype(BF)
-        top = jnp.concatenate([none, none, mm(x, fold), none], axis=1).astype(BF)
-        x = mc[s].astype(F32)
-        middle = jnp.concatenate([x[:, 0, :], x[:, 1, :], none, none], axis=1).astype(BF)
-        for n, x in enumerate((middle, middle, top, top)):
-            wide[s * 128 + n * 32 : s * 128 + n * 32 + 32, :] = x
-    mtf = mt[...].astype(F32)
-    for j in range(2):
-        down[j] = mtf[:, j, :].T.astype(BF)
-
 
 def spread_kernel(got, meta, near_got, far_got, out):
     x = got[...]
-    for n in range(32):
+    for n in range(16):
         out[n] = x
 
 
@@ -321,7 +318,7 @@
     lane = iota((8, 128), 1) // 32
 
     def block(d):
-        return got[(d >> 6) * 64 + (d & 7) * 8 + ((d >> 3) & 7)].astype(F32)
+        return got[(d >> 6) * 64 + ((d >> 1) & 3) * 16 + ((d >> 3) & 7) * 2 + (d & 1)].astype(F32)
 
     rows = [[], [], []]
     for s in range(8):
@@ -393,7 +390,7 @@
     payload, near_msg, far_msg, lc, cl, basis, lt, ct, mt = pl.pallas_call(
         upward_kernel,
         out_shape=(
-            S((8, 8, 128), BF), S((80, 128), BF), S((80, 128), BF), S((32, 1024), BF), S((32, 128), BF),
+            S((16, 8, 128), BF), S((80, 128), BF), S((80, 128), BF), S((32, 1024), BF), S((32, 128), BF),
             S((32, 8192), BF), S((32, 32, 128), BF), S((512, 32), BF), S((32, 2, 32), BF),
         ),
         in_specs=[hbm()] * 5,
@@ -407,28 +404,28 @@
     def device_id(x, z, y, c):
         return ((x * 8 + z) * 4 + y) * 2 + c
 
-    rest = [(x, y, c) for x in range(4) for y in range(4) for c in range(2)]
-    along_z = [[device_id(x, z, y, c) for z in range(8)] for x, y, c in rest]
-    across = [[device_id(x, z, y, c) for x, y, c in rest] for z in range(8)]
+    flat = [(x, y) for x in range(4) for y in range(4)]
+    deep = [(z, c) for z in range(8) for c in range(2)]
+    along_z = [[device_id(x, z, y, c) for z, c in deep] for x, y in flat]
+    across = [[device_id(x, z, y, c) for x, y in flat] for z, c in deep]
     got = lax.all_to_all(payload, "rows", 0, 0, axis_index_groups=along_z, tiled=True)
 
     far_got = lax.ppermute(
-        far_msg, "rows", [(i, ((i + 1) ^ 1) - 1) for i in range(1, 255)]
+        far_msg, "rows", [(i, (((i + 1) ^ 1) - 1) % 256) for i in range(256)]
     )
     near_got = lax.ppermute(near_msg, "rows", [(i, i ^ 1) for i in range(256)])
 
-    bases, nidx, rel, crel, meta = pl.pallas_call(
+    bases, leaf_bases, nidx, rel, crel, meta = pl.pallas_call(
         compose_kernel,
         out_shape=(
-            S((32, 8192), BF), S((6, 128), I32), S((8, 128), I32), S((128, 8), I32), S((24, 128), I32),
+            S((32, 8192), BF), S((32, 8192), BF), S((6, 128), I32), S((8, 128), I32), S((128, 8), I32), S((24, 128), I32),
         ),
         in_specs=[vm()] * 3 + [hbm()] * 8,
-        out_specs=(vm(),) * 5,
+        out_specs=(vm(),) * 6,
         scratch_shapes=[
             V((6, 128), I32), V((128,), I32), V((8, 128), I32), V((3, 16), I32), V((16,), I32),
             pltpu.SMEM((2, 8), I32), pltpu.SMEM((2,), I32), V((8, 64), I32),
-            V((1024, 128), F32), V((512, 128), F32), V((4096, 128), F32), V((32, 8192), BF),
-            DMA((8,)),
+            V((1024, 128), F32), V((512, 128), F32), V((4096, 128), F32), DMA((8,)),
         ],
         compiler_params=params(16),
         cost_estimate=cost(10**9, 2 * MIB),
@@ -446,38 +443,38 @@
 
     got = pl.pallas_call(
         spread_kernel,
-        out_shape=S((32, 64, 128), BF),
+        out_shape=S((16, 128, 128), BF),
         in_specs=[vm()] * 4,
         out_specs=vm(),
         compiler_params=params(16),
         cost_estimate=cost(10**5, MIB // 2),
         name="spread",
-    )(got.reshape(64, 128), meta, near_got, far_got)
+    )(got.reshape(128, 128), meta, near_got, far_got)
     got = lax.all_to_all(got, "rows", 0, 0, axis_index_groups=across, tiled=True)
     got = got.reshape(256, 8, 128)
 
     total, tables, down = pl.pallas_call(
         field_kernel,
         out_shape=(S((8, 8192), F32), S((1024, 128), BF), S((2, 32, 32), BF)),
-        in_specs=[sm()] + [vm()] * 7 + [hbm()] * 8,
+        in_specs=[sm()] + [vm()] * 8 + [hbm()] * 7,
         out_specs=(vm(),) * 3,
         scratch_shapes=[
             V((80, 128), BF), V((80, 128), BF), V((8, 8192), BF), V((8, 6, 64, 1024), BF),
-            V((8, 32, 32, 128), BF), V((3, 32, 16, 32), BF), V((32, 32, 128), BF), V((32, 8192), BF),
+            V((8, 32, 32, 128), BF), V((3, 32, 16, 32), BF), V((32, 8192), BF),
             V((8, 32, 32, 64), BF), V((8, 32, 2, 32), BF),
-            V((8, 256, 128), F32), V((1024, 128), F32), V((256, 128), F32), V((1024, 128), F32),
-            V((137, 8, 128), F32), DMA((22,)),
+            V((8, 256, 128), F32), V((128, 128), F32), V((1024, 128), F32),
+            V((137, 8, 128), F32), DMA((28,)),
         ],
         compiler_params=params(32),
         cost_estimate=cost(2 * 10**9, 12 * MIB),
         name="field",
     )(
-        nidx, rel, crel, lc, cl, near_got, far_got, mt,
+        nidx, rel, crel, lc, cl, near_got, far_got, mt, leaf_bases,
         *map(
             far_away,
             (
                 vectors, near_block, leaf_coupling, jnp.transpose(cluster_coupling, (0, 1, 3, 2)),
-                leaf_trans, basis_leaf, top_coupling, jnp.transpose(middle_coupling, (0, 1, 3, 2)),
+                basis_leaf, top_coupling, jnp.transpose(middle_coupling, (0, 1, 3, 2)),
             ),
         ),
     )

time: 43.4 us -> 41.4 us (0.954)
  starting transfers between devices: 22.2 us -> 18.4 us
  waiting for transfers between devices: 0.92 us -> 2.93 us
    all_to_all x1, waiting for transfers between devices: 0.01 us -> 2.4 us  [body(): lax.all_to_all(payload, 'rows', 0, 0, axis_index_groups=along_z, tiled=True)]
    all_to_all x1, starting transfers between devices: 9.12 us -> 6.75 us  [body(): lax.all_to_all(got, 'rows', 0, 0, axis_index_groups=across, tiled=True)]
    ppermute x1, starting transfers between devices: 3.09 us -> 1.5 us  [body(): lax.ppermute(far_msg, 'rows', [(i, ((i + 1 ^ 1) - 1) % 256) for i in rang...]
    all_to_all x1, starting transfers between devices: 9.02 us -> 9.99 us  [body(): lax.all_to_all(payload, 'rows', 0, 0, axis_index_groups=along_z, tiled=True)]
    pallas_call x1, Pallas kernels: 10.7 us -> 9.81 us  [body(): pl.pallas_call(field_kernel, out_shape=(S((8, 8192), F32), S((1024, 128),...]
    ppermute x1, starting transfers between devices: 0.96 us -> 0.19 us  [body(): near_got = lax.ppermute(near_msg, 'rows', [(i, i ^ 1) for i in range(256)])]
    pallas_call x3, Pallas kernels: 6.9 us -> 7.58 us  [the longest x1 3.4 us: body(): pl.pallas_call(upward_kernel, out_shape=(S((16, 8, 128), BF), S((80, 128)...]
  transfers between devices with their start and end apart: 4 -> 4, of which waited for: 1 -> 2; matrix products, arithmetic and copies ran while one was open for 0% -> 0% of each run, Pallas kernels for 31% -> 32%
where the time goes in v2:
time: 41.4 us; the launch traced here: 41.1 us
  Pallas kernels  19.7 us (48%)
  starting transfers between devices  18.4 us (44%)
  waiting for transfers between devices  2.93 us (7%)
    all_to_all x1, starting transfers between devices, body(): lax.all_to_all(payload, 'rows', 0, 0, axis_index_groups=along_z, tiled=True)  9.99 us
    pallas_call x1, Pallas kernels, body(): pl.pallas_call(field_kernel, out_shape=(S((8, 8192), F32), S((1024, 128),...  9.81 us
    all_to_all x1, starting transfers between devices, body(): lax.all_to_all(got, 'rows', 0, 0, axis_index_groups=across, tiled=True)  6.75 us
    pallas_call x1, Pallas kernels, body(): pl.pallas_call(upward_kernel, out_shape=(S((16, 8, 128), BF), S((80, 128)...  3.4 us
    pallas_call x1, Pallas kernels, body(): pl.pallas_call(compose_kernel, out_shape=(S((32, 8192), BF), S((32, 8192)...  3.27 us
    all_to_all x1, waiting for transfers between devices, body(): lax.all_to_all(payload, 'rows', 0, 0, axis_index_groups=along_z, tiled=True)  2.4 us
    pallas_call x1, Pallas kernels, body(): pl.pallas_call(tail_kernel, out_shape=S((8, 8192), BF), in_specs=[sm()] +...  2.3 us
    ppermute x1, starting transfers between devices, body(): lax.ppermute(far_msg, 'rows', [(i, ((i + 1 ^ 1) - 1) % 256) for i in rang...  1.5 us
  transfers between devices with their start and end apart: 4, of which 2 were waited for; matrix products, arithmetic and copies ran while one was open for 0% of the time, Pallas kernels for 32%

profile of v2, /device:TPU:1, one launch (start us, length us, event | category | flops | bytes accessed | tf_op | source)
XLA Modules:
  0.0 41.1 jit_solution(12152200850943674559)
XLA Ops:
  0.0 3.4 %upward.1 = (bf16[16,8,128]{2,1,0:T(8,128)(2,1)}, bf16[80,128]{1,0:T(8,128)(2,1)S(1)}, bf16[80,128]{1,0:T(8,128)(2,1)S(1)}, bf16[32,1024]{1,0:T(8,128)(2,1)S(1)}...) custom-call(bf16[8,8192]{1,0:T(8,128)(2,1)} %vec_h.3, ...), custom_call_target="tpu_custom_call" | custom-call | flops 100000000 | bytes 1048576 | tf_op jit(solution)/shard_map/upward/pallas_call | solution.py:390
  3.4 10.0 %all-to-all-start = ((bf16[16,8,128]{2,1,0:T(8,128)(2,1)}), bf16[16,8,128]{2,1,0:T(8,128)(2,1)S(1)}, u32[]{:S(2)}, u32[]{:S(2)}) async-start(bf16[16,8,128]{2,1,0:T(8,128)(2,1)} %get-tuple-element.27), calls=%async_computation | async-start | bytes 65536 | tf_op jit(solution)/shard_map/all_to_all | solution.py:411
  13.4 0.2 collective-permute-start
  13.6 1.5 %collective-permute-start.1 = (bf16[80,128]{1,0:T(8,128)(2,1)S(1)}, bf16[80,128]{1,0:T(8,128)(2,1)S(1)}, u32[]{:S(2)}, u32[]{:S(2)}) collective-permute-start(bf16[80,128]{1,0:T(8,128)(2,1)S(1)} %get-tuple-element.29), channel_id=1, source_target_pairs={{0,255},{1,2},{2,1},{3,4},{4,3},{5,6},{6,5},{7,8},{8,7},{9,10},{10... | collective-permute-start | bytes 61448 | tf_op jit(solution)/shard_map/ppermute | solution.py:413
  15.1 3.3 %compose.1 = (bf16[32,8192]{1,0:T(8,128)(2,1)S(1)}, bf16[32,8192]{1,0:T(8,128)(2,1)S(1)}, s32[6,128]{1,0:T(8,128)S(1)}, s32[8,128]{1,0:T(8,128)S(1)}, s32[128,8]{1,0:T(8,128)S(1)}, /*index=5*/s32[24,128]{1,0:T(8,128)S(1)}) custom-call(bf16[32,32,128]{2,1,0:T(8,128)(2,1)S(1)} %get-tuple-element.23.lt, bf16[32,8192]{1,0:T(8,128)(2,1)S(1)} %get-tuple-element.24.basis, ...), custom_call_target="tpu_custom_call" | custom-call | flops 1000000000 | bytes 2097152 | tf_op jit(solution)/shard_map/compose/pallas_call | solution.py:418
  18.4 0.0 collective-permute-done.near_got
  18.4 0.0 collective-permute-done.1.far_got
  18.4 2.4 %all-to-all-done = bf16[16,8,128]{2,1,0:T(8,128)(2,1)S(1)} async-done(((bf16[16,8,128]{2,1,0:T(8,128)(2,1)}), bf16[16,8,128]{2,1,0:T(8,128)(2,1)S(1)}, u32[]{:S(2)}, u32[]{:S(2)}) %all-to-all-start) | async-done | bytes 32800 | tf_op jit(solution)/shard_map/all_to_all | solution.py:411
  20.8 0.9 %spread.1 = bf16[16,128,128]{2,1,0:T(8,128)(2,1)} custom-call(bf16[128,128]{1,0:T(8,128)(2,1)S(1)} %bitcast.10, s32[24,128]{1,0:T(8,128)S(1)} %get-tuple-element.26.meta, bf16[80,128]{1,0:T(8,128)(2,1)S(1)} %collective-permute-done.near_got, bf16[80,128]{1,0:T(8,128)(2,1)S(1)} %collective-permute-done.1.far_got), custom_call_target="tpu_custom_call" | custom-call | flops 100000 | bytes 524288 | tf_op jit(solution)/shard_map/spread/pallas_call | solution.py:444
  21.7 6.8 %all-to-all-start.1 = ((bf16[16,128,128]{2,1,0:T(8,128)(2,1)}), bf16[16,128,128]{2,1,0:T(8,128)(2,1)S(1)}, u32[]{:S(2)}, u32[]{:S(2)}) async-start(bf16[16,128,128]{2,1,0:T(8,128)(2,1)} %spread.1), calls=%async_computation.1 | async-start | bytes 1048576 | tf_op jit(solution)/shard_map/all_to_all | solution.py:453
  28.5 9.8 %field.1 = (f32[8,8192]{1,0:T(8,128)S(1)}, bf16[1024,128]{1,0:T(8,128)(2,1)S(1)}, bf16[2,32,32]{2,1,0:T(8,128)(2,1)S(1)}) custom-call(s32[6,128]{1,0:T(8,128)S(1)} %get-tuple-element.30.nidx, s32[8,128]{1,0:T(8,128)S(1)} %get-tuple-element.31.rel, s32[128,8]{1,0:T(8,128)S(1)} %get-tuple-element.32.crel, bf16[32,1024]{1,0:T(8,128)(2,1)S(1)} %get-tuple-element.33.lc, ...), custom_call_target="tpu_custom_call" | custom-call | flops 2000000000 | bytes 12582912 | tf_op jit(solution)/shard_map/field/pallas_call | solution.py:456
  38.3 0.5 %all-to-all-done.1 = bf16[16,128,128]{2,1,0:T(8,128)(2,1)S(1)} async-done(((bf16[16,128,128]{2,1,0:T(8,128)(2,1)}), bf16[16,128,128]{2,1,0:T(8,128)(2,1)S(1)}, u32[]{:S(2)}, u32[]{:S(2)}) %all-to-all-start.1) | async-done | bytes 524320 | tf_op jit(solution)/shard_map/all_to_all | solution.py:453
  38.8 2.3 %tail.1 = bf16[8,8192]{1,0:T(8,128)(2,1)} custom-call(s32[24,128]{1,0:T(8,128)S(1)} %get-tuple-element.26.meta, bf16[256,8,128]{2,1,0:T(8,128)(2,1)S(1)} %bitcast.9, bf16[1024,128]{1,0:T(8,128)(2,1)S(1)} %get-tuple-element.37.wm, bf16[2,32,32]{2,1,0:T(8,128)(2,1)S(1)} %get-tuple-element.38.down, f32[8,8192]{1,0:T(8,128)S(1)} %get-tuple-element.39.total, ...), custom_call_target="tpu_custom_call" | custom-call | flops 100000000 | bytes 2097152 | tf_op jit(solution)/shard_map/tail/pallas_call | solution.py:482
Async XLA Ops:
  3.4 17.4 %all-to-all-start = ((bf16[16,8,128]{2,1,0:T(8,128)(2,1)}), bf16[16,8,128]{2,1,0:T(8,128)(2,1)S(1)}, u32[]{:S(2)}, u32[]{:S(2)}) async-start(bf16[16,8,128]{2,1,0:T(8,128)(2,1)} %get-tuple-element.27), calls=%async_computation | async-start | bytes 65536 | tf_op jit(solution)/shard_map/all_to_all | solution.py:411
  13.4 5.0 %collective-permute-start = (bf16[80,128]{1,0:T(8,128)(2,1)S(1)}, bf16[80,128]{1,0:T(8,128)(2,1)S(1)}, u32[]{:S(2)}, u32[]{:S(2)}) collective-permute-start(bf16[80,128]{1,0:T(8,128)(2,1)S(1)} %get-tuple-element.28), channel_id=1, source_target_pairs={{0,1},{1,0},{2,3},{3,2},{4,5},{5,4},{6,7},{7,6},{8,9},{9,8},{10,11... | collective-permute-start | bytes 61448 | tf_op jit(solution)/shard_map/ppermute | solution.py:416
  13.6 4.8 %collective-permute-start.1 = (bf16[80,128]{1,0:T(8,128)(2,1)S(1)}, bf16[80,128]{1,0:T(8,128)(2,1)S(1)}, u32[]{:S(2)}, u32[]{:S(2)}) collective-permute-start(bf16[80,128]{1,0:T(8,128)(2,1)S(1)} %get-tuple-element.29), channel_id=1, source_target_pairs={{0,255},{1,2},{2,1},{3,4},{4,3},{5,6},{6,5},{7,8},{8,7},{9,10},{10... | collective-permute-start | bytes 61448 | tf_op jit(solution)/shard_map/ppermute | solution.py:413
  21.7 17.1 %all-to-all-start.1 = ((bf16[16,128,128]{2,1,0:T(8,128)(2,1)}), bf16[16,128,128]{2,1,0:T(8,128)(2,1)S(1)}, u32[]{:S(2)}, u32[]{:S(2)}) async-start(bf16[16,128,128]{2,1,0:T(8,128)(2,1)} %spread.1), calls=%async_computation.1 | async-start | bytes 1048576 | tf_op jit(solution)/shard_map/all_to_all | solution.py:453

commit v3 on v2

--- a/solution.py
+++ b/solution.py
@@ -45,7 +45,7 @@
     even = lax.axis_index("rows") % 2 == 0
     own = (iota((32, 256), 1) // 64 == iota((32, 256), 0) // 8).astype(F32)
     eye = (iota((32, 32), 0) == iota((32, 32), 1)).astype(BF)
-    for copy in copies[:3]:
+    for copy in copies:
         copy.wait()
     mtf = mt[...].astype(F32)
     mtj = [mtf[:, j, :].astype(BF) for j in range(2)]
@@ -63,7 +63,6 @@
         first = jnp.where(group == v, pltpu.roll(x, v * 16, 1) if v else x, first)
         last = jnp.where(group == v, pltpu.roll(x, v * 16 + 16, 1) if v < 7 else x, last)
     lc[...] = lcs[...].astype(BF)
-    copies[3].wait()
     sums = [jnp.zeros((32, 128), F32) for _ in range(8)]
     for r in range(32):
         w = lt[r].astype(F32)
@@ -80,7 +79,6 @@
     gather = (iota((8, 256), 0) == iota((8, 256), 1) // 32).astype(BF)
     y = mm(gather, y)
     half = iota((8, 512), 1) % 16 // 8
-    copies[4].wait()
     pieces = []
     top = jnp.zeros((8, 32), F32)
     for j in range(2):
@@ -155,19 +153,12 @@
     total, wide, down,
     ml, mr, vec, nb, coup, ccoup, basis, tc, mc, picked, partial, rows, tiles, sems,
 ):
-    order = [(vec_h, vec), (ccoup_h, ccoup), (mc_h, mc)]
-    for s in range(8):
-        order.append((coup_h.at[s], coup.at[s]))
-        order.append((nb_h.at[:, :, pl.ds(s * 1024, 1024)], nb.at[s]))
-        order.append((tc_h.at[s], tc.at[s]))
-    order.append((basis_h, basis))
-    copies = [pltpu.make_async_copy(a, b, sems.at[n]) for n, (a, b) in enumerate(order)]
-
-    def start(first, last):
-        for copy in copies[first:last]:
-            copy.start()
-
-    start(0, 9)
+    near_parts = [(nb_h.at[:, :, pl.ds(n * 2048, 2048)], nb.at[n]) for n in range(4)]
+    order = [
+        (vec_h, vec), (ccoup_h, ccoup), (coup_h, coup), *near_parts[:2],
+        (mc_h, mc), (tc_h, tc), *near_parts[2:], (basis_h, basis),
+    ]
+    copies = fetch(sems, *order)
     even = lax.axis_index("rows") % 2 == 0
     a, b = near_got[...].astype(F32), far_got[...].astype(F32)
     ml[...] = jnp.where(even, b, a).astype(BF)
@@ -198,7 +189,8 @@
         tiles[at] = jnp.where(low, x, y)
         tiles[at + 1] = jnp.where(low, y, x)
 
-    copies[0].wait()
+    for copy in copies[0:3]:
+        copy.wait()
     for p in range(64):
         put(vec[:, p * 128 : (p + 1) * 128].astype(F32), 4 + 2 * p)
     for ref, at in ((ml, 0), (mr, 132)):
@@ -222,7 +214,6 @@
             partners.append(mm_nt(onehot, clhs).astype(BF))
 
     def cluster_couple():
-        copies[1].wait()
         field = jnp.zeros((128, 32), F32)
         for s in range(3):
             x = jnp.where(own, mm(partners[s], spread), 0.0).astype(BF)
@@ -251,45 +242,49 @@
         wide[s * 128 : s * 128 + 32, :] = middle
         wide[s * 128 + 32 : s * 128 + 64, :] = middle
 
-    sums = [jnp.zeros((32, 128), F32) for _ in range(8)]
-    for t in range(32):
-        s, p0 = t // 4, t % 4 * 8
-        if t % 4 == 0:
-            for copy in copies[3 + s * 3 : 6 + s * 3]:
-                copy.wait()
-            if s < 7:
-                start(9 + s * 3, min(12 + s * 3, 28))
-        for p in range(p0, p0 + 8):
-            w = coup[s, p].astype(F32)
-            sums = [sums[v] + w * picked[s, v * 32 + p : v * 32 + p + 1, :] for v in range(8)]
+    def near_part(n):
         parts = []
         for l in range(4):
-            i = t * 4 + l
+            i = n * 4 + l
             parts.append(
                 jnp.concatenate(
                     [
-                        jnp.where(low, tiles[nidx[2 * n, i]], tiles[nidx[2 * n + 1, i]])
-                        for n in range(3)
+                        jnp.where(low, tiles[nidx[2 * m, i]], tiles[nidx[2 * m + 1, i]])
+                        for m in range(3)
                     ],
                     axis=1,
                 )
             )
         x = jnp.concatenate(parts, axis=0).astype(BF)
-        a, c = t * 256, t % 4 * 256
-        r = mm(x, nb[s, :, :, c : c + 256].reshape(384, 256))
+        a, c = n * 256, n % 8 * 256
+        r = mm(x, nb[n // 8, :, :, c : c + 256].reshape(384, 256))
         total[:, a : a + 128] = jnp.where(low, r[0:8, 0:128], r[8:16, 0:128])
         total[:, a + 128 : a + 256] = jnp.where(low, r[16:24, 128:256], r[24:32, 128:256])
-        if t % 4 == 1:
-            top_table(s)
+
+    sums = [jnp.zeros((32, 128), F32) for _ in range(8)]
+    for t in range(32):
+        s, p0 = t // 4, t % 4 * 8
+        if t == 16:
+            for copy in copies[3:7]:
+                copy.wait()
+        if t == 24:
+            for copy in copies[7:10]:
+                copy.wait()
+        for p in range(p0, p0 + 8):
+            w = coup[s, p].astype(F32)
+            sums = [sums[v] + w * picked[s, v * 32 + p : v * 32 + p + 1, :] for v in range(8)]
+        for n in (2 * t - 32, 2 * t - 31) if t >= 16 else ():
+            near_part(n)
+        if t >= 16 and t % 2 == 1:
+            top_table((t - 16) // 2)
         if t == 2:
             cluster_pick()
         if t == 6:
             cluster_couple()
         if t == 10:
             cluster_store()
-            copies[2].wait()
-        if t >= 11 and t % 2 == 0 and t < 27:
-            middle_table((t - 12) // 2)
+        if t >= 16 and t % 2 == 0:
+            middle_table((t - 16) // 2)
 
     mtf = mt[...].astype(F32)
     for j in range(2):
@@ -297,7 +292,6 @@
     eye = (iota((128, 128), 0) == iota((128, 128), 1)).astype(BF)
     for v in range(8):
         rows[pl.ds(v, 128, stride=8), 0:32] = mm_nt(eye, sums[v].astype(BF))
-    copies[27].wait()
     for k in range(16):
         x = partial[pl.ds(k, 8, stride=16), :][:, 0:32].astype(BF)
         here = slice(k * 512, (k + 1) * 512)
@@ -411,7 +405,7 @@
     got = lax.all_to_all(payload, "rows", 0, 0, axis_index_groups=along_z, tiled=True)
 
     far_got = lax.ppermute(
-        far_msg, "rows", [(i, (((i + 1) ^ 1) - 1) % 256) for i in range(256)]
+        far_msg, "rows", [(0, 0), (255, 255)] + [(i, ((i + 1) ^ 1) - 1) for i in range(1, 255)]
     )
     near_got = lax.ppermute(near_msg, "rows", [(i, i ^ 1) for i in range(256)])
 
@@ -459,11 +453,11 @@
         in_specs=[sm()] + [vm()] * 8 + [hbm()] * 7,
         out_specs=(vm(),) * 3,
         scratch_shapes=[
-            V((80, 128), BF), V((80, 128), BF), V((8, 8192), BF), V((8, 6, 64, 1024), BF),
+            V((80, 128), BF), V((80, 128), BF), V((8, 8192), BF), V((4, 6, 64, 2048), BF),
             V((8, 32, 32, 128), BF), V((3, 32, 16, 32), BF), V((32, 8192), BF),
             V((8, 32, 32, 64), BF), V((8, 32, 2, 32), BF),
             V((8, 256, 128), F32), V((128, 128), F32), V((1024, 128), F32),
-            V((137, 8, 128), F32), DMA((28,)),
+            V((137, 8, 128), F32), DMA((10,)),
         ],
         compiler_params=params(32),
         cost_estimate=cost(2 * 10**9, 12 * MIB),

time: 41.4 us -> 41.9 us (1.012)
  the two profiles are of different devices: /device:TPU:1 before, /device:TPU:33 now
where the time goes in v3:
time: 41.9 us; the launch traced here: 41.6 us
  starting transfers between devices  19.7 us (47%)
  Pallas kernels  18.8 us (45%)
  waiting for transfers between devices  3.01 us (7%)
    pallas_call x1, Pallas kernels, body(): pl.pallas_call(field_kernel, out_shape=(S((8, 8192), F32), S((1024, 128),...  9.02 us
    all_to_all x1, starting transfers between devices, body(): lax.all_to_all(payload, 'rows', 0, 0, axis_index_groups=along_z, tiled=True)  8.91 us
    all_to_all x1, starting transfers between devices, body(): lax.all_to_all(got, 'rows', 0, 0, axis_index_groups=across, tiled=True)  7.23 us
    pallas_call x1, Pallas kernels, body(): pl.pallas_call(upward_kernel, out_shape=(S((16, 8, 128), BF), S((80, 128)...  3.28 us
    pallas_call x1, Pallas kernels, body(): pl.pallas_call(compose_kernel, out_shape=(S((32, 8192), BF), S((32, 8192)...  3.28 us
    ppermute x1, starting transfers between devices, body(): lax.ppermute(far_msg, 'rows', [(0, 0), (255, 255)] + [(i, (i + 1 ^ 1) - 1...  3.23 us
    all_to_all x1, waiting for transfers between devices, body(): lax.all_to_all(got, 'rows', 0, 0, axis_index_groups=across, tiled=True)  3.01 us
    pallas_call x1, Pallas kernels, body(): pl.pallas_call(tail_kernel, out_shape=S((8, 8192), BF), in_specs=[sm()] +...  2.3 us
  transfers between devices with their start and end apart: 4, of which 1 were waited for; matrix products, arithmetic and copies ran while one was open for 0% of the time, Pallas kernels for 30%

profile of v3, /device:TPU:33, one launch (start us, length us, event | category | flops | bytes accessed | tf_op | source)
XLA Modules:
  0.0 41.6 jit_solution(6905288733364189514)
XLA Ops:
  0.0 3.3 %upward.1 = (bf16[16,8,128]{2,1,0:T(8,128)(2,1)}, bf16[80,128]{1,0:T(8,128)(2,1)S(1)}, bf16[80,128]{1,0:T(8,128)(2,1)S(1)}, bf16[32,1024]{1,0:T(8,128)(2,1)S(1)}...) custom-call(bf16[8,8192]{1,0:T(8,128)(2,1)} %vec_h.3, ...), custom_call_target="tpu_custom_call" | custom-call | flops 100000000 | bytes 1048576 | tf_op jit(solution)/shard_map/upward/pallas_call | solution.py:384
  3.3 8.9 %all-to-all-start = ((bf16[16,8,128]{2,1,0:T(8,128)(2,1)}), bf16[16,8,128]{2,1,0:T(8,128)(2,1)S(1)}, u32[]{:S(2)}, u32[]{:S(2)}) async-start(bf16[16,8,128]{2,1,0:T(8,128)(2,1)} %get-tuple-element.27), calls=%async_computation | async-start | bytes 65536 | tf_op jit(solution)/shard_map/all_to_all | solution.py:405
  12.2 0.4 collective-permute-start
  12.6 3.2 %collective-permute-start.1 = (bf16[80,128]{1,0:T(8,128)(2,1)S(1)}, bf16[80,128]{1,0:T(8,128)(2,1)S(1)}, u32[]{:S(2)}, u32[]{:S(2)}) collective-permute-start(bf16[80,128]{1,0:T(8,128)(2,1)S(1)} %get-tuple-element.29), channel_id=1, source_target_pairs={{0,0},{255,255},{1,2},{2,1},{3,4},{4,3},{5,6},{6,5},{7,8},{8,7},{9... | collective-permute-start | bytes 61448 | tf_op jit(solution)/shard_map/ppermute | solution.py:407
  15.8 3.3 %compose.1 = (bf16[32,8192]{1,0:T(8,128)(2,1)S(1)}, bf16[32,8192]{1,0:T(8,128)(2,1)S(1)}, s32[6,128]{1,0:T(8,128)S(1)}, s32[8,128]{1,0:T(8,128)S(1)}, s32[128,8]{1,0:T(8,128)S(1)}, /*index=5*/s32[24,128]{1,0:T(8,128)S(1)}) custom-call(bf16[32,32,128]{2,1,0:T(8,128)(2,1)S(1)} %get-tuple-element.23.lt, bf16[32,8192]{1,0:T(8,128)(2,1)S(1)} %get-tuple-element.24.basis, ...), custom_call_target="tpu_custom_call" | custom-call | flops 1000000000 | bytes 2097152 | tf_op jit(solution)/shard_map/compose/pallas_call | solution.py:412
  19.1 0.0 collective-permute-done.near_got
  19.1 0.0 collective-permute-done.1.far_got
  19.1 0.0 all-to-all-done
  19.1 0.9 %spread.1 = bf16[16,128,128]{2,1,0:T(8,128)(2,1)} custom-call(bf16[128,128]{1,0:T(8,128)(2,1)S(1)} %bitcast.10, s32[24,128]{1,0:T(8,128)S(1)} %get-tuple-element.26.meta, bf16[80,128]{1,0:T(8,128)(2,1)S(1)} %collective-permute-done.near_got, bf16[80,128]{1,0:T(8,128)(2,1)S(1)} %collective-permute-done.1.far_got), custom_call_target="tpu_custom_call" | custom-call | flops 100000 | bytes 524288 | tf_op jit(solution)/shard_map/spread/pallas_call | solution.py:438
  20.0 7.2 %all-to-all-start.1 = ((bf16[16,128,128]{2,1,0:T(8,128)(2,1)}), bf16[16,128,128]{2,1,0:T(8,128)(2,1)S(1)}, u32[]{:S(2)}, u32[]{:S(2)}) async-start(bf16[16,128,128]{2,1,0:T(8,128)(2,1)} %spread.1), calls=%async_computation.1 | async-start | bytes 1048576 | tf_op jit(solution)/shard_map/all_to_all | solution.py:447
  27.3 9.0 %field.1 = (f32[8,8192]{1,0:T(8,128)S(1)}, bf16[1024,128]{1,0:T(8,128)(2,1)S(1)}, bf16[2,32,32]{2,1,0:T(8,128)(2,1)S(1)}) custom-call(s32[6,128]{1,0:T(8,128)S(1)} %get-tuple-element.30.nidx, s32[8,128]{1,0:T(8,128)S(1)} %get-tuple-element.31.rel, s32[128,8]{1,0:T(8,128)S(1)} %get-tuple-element.32.crel, bf16[32,1024]{1,0:T(8,128)(2,1)S(1)} %get-tuple-element.33.lc, ...), custom_call_target="tpu_custom_call" | custom-call | flops 2000000000 | bytes 12582912 | tf_op jit(solution)/shard_map/field/pallas_call | solution.py:450
  36.3 3.0 %all-to-all-done.1 = bf16[16,128,128]{2,1,0:T(8,128)(2,1)S(1)} async-done(((bf16[16,128,128]{2,1,0:T(8,128)(2,1)}), bf16[16,128,128]{2,1,0:T(8,128)(2,1)S(1)}, u32[]{:S(2)}, u32[]{:S(2)}) %all-to-all-start.1) | async-done | bytes 524320 | tf_op jit(solution)/shard_map/all_to_all | solution.py:447
  39.3 2.3 %tail.1 = bf16[8,8192]{1,0:T(8,128)(2,1)} custom-call(s32[24,128]{1,0:T(8,128)S(1)} %get-tuple-element.26.meta, bf16[256,8,128]{2,1,0:T(8,128)(2,1)S(1)} %bitcast.9, bf16[1024,128]{1,0:T(8,128)(2,1)S(1)} %get-tuple-element.37.wm, bf16[2,32,32]{2,1,0:T(8,128)(2,1)S(1)} %get-tuple-element.38.down, f32[8,8192]{1,0:T(8,128)S(1)} %get-tuple-element.39.total, ...), custom_call_target="tpu_custom_call" | custom-call | flops 100000000 | bytes 2097152 | tf_op jit(solution)/shard_map/tail/pallas_call | solution.py:476
Async XLA Ops:
  3.3 15.8 %all-to-all-start = ((bf16[16,8,128]{2,1,0:T(8,128)(2,1)}), bf16[16,8,128]{2,1,0:T(8,128)(2,1)S(1)}, u32[]{:S(2)}, u32[]{:S(2)}) async-start(bf16[16,8,128]{2,1,0:T(8,128)(2,1)} %get-tuple-element.27), calls=%async_computation | async-start | bytes 65536 | tf_op jit(solution)/shard_map/all_to_all | solution.py:405
  12.2 6.9 %collective-permute-start = (bf16[80,128]{1,0:T(8,128)(2,1)S(1)}, bf16[80,128]{1,0:T(8,128)(2,1)S(1)}, u32[]{:S(2)}, u32[]{:S(2)}) collective-permute-start(bf16[80,128]{1,0:T(8,128)(2,1)S(1)} %get-tuple-element.28), channel_id=1, source_target_pairs={{0,1},{1,0},{2,3},{3,2},{4,5},{5,4},{6,7},{7,6},{8,9},{9,8},{10,11... | collective-permute-start | bytes 61448 | tf_op jit(solution)/shard_map/ppermute | solution.py:410
  12.6 6.5 %collective-permute-start.1 = (bf16[80,128]{1,0:T(8,128)(2,1)S(1)}, bf16[80,128]{1,0:T(8,128)(2,1)S(1)}, u32[]{:S(2)}, u32[]{:S(2)}) collective-permute-start(bf16[80,128]{1,0:T(8,128)(2,1)S(1)} %get-tuple-element.29), channel_id=1, source_target_pairs={{0,0},{255,255},{1,2},{2,1},{3,4},{4,3},{5,6},{6,5},{7,8},{8,7},{9... | collective-permute-start | bytes 61448 | tf_op jit(solution)/shard_map/ppermute | solution.py:407
  20.0 19.3 %all-to-all-start.1 = ((bf16[16,128,128]{2,1,0:T(8,128)(2,1)}), bf16[16,128,128]{2,1,0:T(8,128)(2,1)S(1)}, u32[]{:S(2)}, u32[]{:S(2)}) async-start(bf16[16,128,128]{2,1,0:T(8,128)(2,1)} %spread.1), calls=%async_computation.1 | async-start | bytes 1048576 | tf_op jit(solution)/shard_map/all_to_all | solution.py:447
